TPU v7x, 128 devices: a whole 4x4x4 slice. The times are simulated.
128 devices in a mesh: outer: 16 (over y, x_hi, core), inner: 8 (over z, x_lo).
Axes of the slice: x: 4 (x_hi: 2, x_lo: 2; x = x_hi * 2 + x_lo), y: 4, z: 4, core: 2. Of those that a mesh axis runs over, the one named last changes fastest.
Arguments:
- queries: bfloat16 [14336, 4096], P(('outer', 'inner')), may hold values from -130 to 130
- keys: bfloat16 [14336, 512], P(('outer', 'inner')), may hold values from -5.1 to 5.1
- values: bfloat16 [14336, 512], P(('outer', 'inner')), may hold values from -6 to 6
- positions: int32 [14336], P(('outer', 'inner')), may hold values from 0 to 14335, as said below
Outputs:
- attended: bfloat16 [14336, 4096], P(('outer', 'inner'))
Inputs may be any that keep to these rules, and one draw needn't show every extreme that they name: positions is a permutation of 0 to 14335 made of runs: rows r * 56 to (r + 1) * 56 - 1 hold 56 consecutive positions starting at a multiple of 56, in increasing order.
All inputs are finite; a program needn't handle non-finite values.
Results may differ from a plain program's by a relative error of at most 0.0065.
Values may be sent and summed in bfloat16 or wider, within the bound.
A program may use at most 128 MiB of HBM per device.

v0:
```python
import jax
import jax.numpy as jnp
from jax import lax
from jax.sharding import PartitionSpec as P

HEADS = 32
KV_HEADS = 4
HEAD_DIM = 128
GROUP = 8


def passed_along(array, axis, by):
    count = lax.axis_size(axis)
    return lax.ppermute(array, axis, [(i, (i + by) % count) for i in range(count)])


def make_tile(query_heads, query_pos, score_scale):

    def tile_step(running, key_block, value_block, pos_block):
        running_max, running_total, running_sum = running
        key_count = key_block.shape[0]
        key_heads = key_block.reshape(key_count, KV_HEADS, HEAD_DIM)
        value_heads = value_block.reshape(key_count, KV_HEADS, HEAD_DIM)
        scores = (
            jnp.einsum("qhgd,khd->hgqk", query_heads, key_heads, preferred_element_type=jnp.float32)
            * score_scale
        )
        visible = pos_block[None, :] <= query_pos[:, None]
        masked = jnp.where(visible, scores, -1e30)
        new_max = jnp.maximum(running_max, jnp.max(masked, axis=-1))
        weights = jnp.where(visible, jnp.exp(masked - new_max[..., None]), 0.0)
        rescale = jnp.exp(running_max - new_max)
        new_total = running_total * rescale + jnp.sum(weights, axis=-1)
        product = jnp.einsum(
            "hgqk,khd->hgqd",
            weights.astype(jnp.bfloat16),
            value_heads,
            preferred_element_type=jnp.float32,
        )
        new_sum = running_sum * rescale[..., None] + product
        return (new_max, new_total, new_sum)

    return tile_step


def on_device(queries, keys, values, positions):
    row_count = queries.shape[0]
    score_scale = HEAD_DIM ** (-0.5)
    query_heads = queries.reshape(row_count, KV_HEADS, GROUP, HEAD_DIM)
    every_pos = lax.all_gather(positions, ("outer", "inner"), axis=0, tiled=True)
    tile_step = make_tile(query_heads, positions, score_scale)
    start_running = (
        jnp.full((KV_HEADS, GROUP, row_count), -1e30, jnp.float32),
        jnp.zeros((KV_HEADS, GROUP, row_count), jnp.float32),
        jnp.zeros((KV_HEADS, GROUP, row_count, HEAD_DIM), jnp.float32),
    )
    group_key, group_value = (
        lax.all_gather(keys, "inner", axis=0, tiled=True),
        lax.all_gather(values, "inner", axis=0, tiled=True),
    )
    group_rows = group_key.shape[0]
    outer_count = lax.axis_size("outer")
    own_group = lax.axis_index("outer")

    def block_pos(first_row, count):
        return lax.dynamic_slice_in_dim(every_pos, first_row, count, 0)

    running = tile_step(
        start_running, group_key, group_value, block_pos(own_group * group_rows, group_rows)
    )

    def advance_block(step_index, packed):
        inner_running, block_now = packed
        block_now = passed_along((block_now[0], block_now[1]), "outer", 1)
        source_group = (own_group - step_index) % outer_count
        inner_running = tile_step(
            inner_running,
            block_now[0],
            block_now[1],
            block_pos(source_group * group_rows, group_rows),
        )
        return (inner_running, block_now)

    running, group_block = lax.fori_loop(
        1, outer_count, advance_block, (running, (group_key, group_value))
    )
    running_max, running_total, running_sum = running
    finished = running_sum / running_total[..., None]
    return (
        jnp.transpose(finished, (2, 0, 1, 3))
        .reshape(row_count, HEADS * HEAD_DIM)
        .astype(jnp.bfloat16)
    )


def solution(mesh):
    return jax.shard_map(
        on_device,
        mesh=mesh,
        in_specs=(
            P(("outer", "inner"), None),
            P(("outer", "inner"), None),
            P(("outer", "inner"), None),
            P(("outer", "inner")),
        ),
        out_specs=P(("outer", "inner"), None),
        check_vma=False,
    )
```

profile of v0, /device:TPU:0, one launch (start us, length us, event | category | flops | bytes accessed | tf_op | source)
XLA Modules:
  0.0 647.7 jit_solution(5160569806451673014)
XLA Ops:
  0.8 68.7 %all-reduce = s32[14336]{0:T(1024)S(1)} all-reduce(s32[14336]{0:T(1024)S(1)} %dynamic-update-slice), channel_id=1, replica_groups=mesh['outer'=16,'inner'=8] {'outer','inner'}, use_global_device_ids=true, to_apply=%add | all-reduce | flops 14336 | bytes 114688
  70.4 31.7 %all_gather.10 = bf16[896,512]{1,0:T(8,128)(2,1)S(1)} all-gather(bf16[112,512]{1,0:T(8,128)(2,1)} %param.7), channel_id=1, replica_groups=mesh['outer'=16,'inner'=8] {'inner'}, dimensions={0}, use_global_device_ids=true | all-gather | bytes 1032192 | tf_op jit(solution)/shard_map/all_gather | solution.py:58
  104.7 4.1 fusion.11
  108.9 4.6 copy-done
  113.5 4.1 fusion.13
  117.6 31.2 %all_gather.11 = bf16[896,512]{1,0:T(8,128)(2,1)S(1)} all-gather(bf16[112,512]{1,0:T(8,128)(2,1)S(1)} %copy-done.3), channel_id=1, replica_groups=mesh['outer'=16,'inner'=8] {'inner'}, dimensions={0}, use_global_device_ids=true | all-gather | bytes 1032192 | tf_op jit(solution)/shard_map/all_gather | solution.py:59
  150.0 9.5 %fusion.17 = f32[4,8,112,128]{3,2,1,0:T(8,128)} fusion(bf16[896,4,128,1]{0,2,3,1:T(8,128)(2,1)} %bitcast.20, f32[4,896,112,8]{1,2,3,0:T(8,128)} %copy-done, f32[4,8,112]{2,1,0:T(8,128)S(1)} %broadcast_maximum_fusion, pred[112,896]{1,0:T(8,128)(4,1)S(1)} %broadcast_compare_fusion.1, f32[4,8,112]{2,1,0:T(8,128)S(1)} %get-tuple-element.295), kind=kOutput, calls=%fused_computation.22 | convolution fusion | flops 838598656 | bytes 15726592 | tf_op jit(solution)/shard_map/hgqk,khd->hgqd/dot_general | solution.py:34
  159.9 484.2 %while.23 = (s32[]{:T(128)}, f32[4,8,112]{2,1,0:T(8,128)S(1)}, f32[4,8,112]{2,1,0:T(8,128)S(1)}, f32[4,8,112,128]{3,2,1,0:T(8,128)}, bf16[896,512]{0,1:T(8,128)(...) while((s32[]{:T(128)}, f32[4,8,112]{2,1,0:T(8,128)S(1)}, ...), condition=%wide.region_5.6_spmd, body=%wide.region_2.5_spmd.sunk | while | flops 1686938624 | bytes 71290248 | solution.py:84
  162.6 14.0 %collective-permute-done = bf16[896,512]{0,1:T(8,128)(2,1)S(1)} collective-permute-done((bf16[896,512]{0,1:T(8,128)(2,1)}, bf16[896,512]{0,1:T(8,128)(2,1)S(1)}, u32[]{:S(2)}, u32[]{:S(2)}) %collective-permute-start) | collective-permute-done | bytes 917536 | tf_op jit(solution)/shard_map/while/body/eval_jaxpr/ppermute | solution.py:14
  179.1 4.1 fusion.43
  186.4 3.9 multiply_add_fusion.5
  192.8 16.1 %collective-permute-done = bf16[896,512]{0,1:T(8,128)(2,1)S(1)} collective-permute-done((bf16[896,512]{0,1:T(8,128)(2,1)}, bf16[896,512]{0,1:T(8,128)(2,1)S(1)}, u32[]{:S(2)}, u32[]{:S(2)}) %collective-permute-start) | collective-permute-done | bytes 917536 | tf_op jit(solution)/shard_map/while/body/eval_jaxpr/ppermute | solution.py:14
  211.4 4.1 fusion.43
  218.7 3.9 multiply_add_fusion.5
  224.8 16.4 %collective-permute-done = bf16[896,512]{0,1:T(8,128)(2,1)S(1)} collective-permute-done((bf16[896,512]{0,1:T(8,128)(2,1)}, bf16[896,512]{0,1:T(8,128)(2,1)S(1)}, u32[]{:S(2)}, u32[]{:S(2)}) %collective-permute-start) | collective-permute-done | bytes 917536 | tf_op jit(solution)/shard_map/while/body/eval_jaxpr/ppermute | solution.py:14
  243.7 4.1 fusion.43
  251.0 3.9 multiply_add_fusion.5
  257.0 16.4 %collective-permute-done = bf16[896,512]{0,1:T(8,128)(2,1)S(1)} collective-permute-done((bf16[896,512]{0,1:T(8,128)(2,1)}, bf16[896,512]{0,1:T(8,128)(2,1)S(1)}, u32[]{:S(2)}, u32[]{:S(2)}) %collective-permute-start) | collective-permute-done | bytes 917536 | tf_op jit(solution)/shard_map/while/body/eval_jaxpr/ppermute | solution.py:14
  275.9 4.1 fusion.43
  283.3 3.9 multiply_add_fusion.5
  289.3 16.4 %collective-permute-done = bf16[896,512]{0,1:T(8,128)(2,1)S(1)} collective-permute-done((bf16[896,512]{0,1:T(8,128)(2,1)}, bf16[896,512]{0,1:T(8,128)(2,1)S(1)}, u32[]{:S(2)}, u32[]{:S(2)}) %collective-permute-start) | collective-permute-done | bytes 917536 | tf_op jit(solution)/shard_map/while/body/eval_jaxpr/ppermute | solution.py:14
  308.2 4.1 fusion.43
  315.5 3.9 multiply_add_fusion.5
  321.6 16.4 %collective-permute-done = bf16[896,512]{0,1:T(8,128)(2,1)S(1)} collective-permute-done((bf16[896,512]{0,1:T(8,128)(2,1)}, bf16[896,512]{0,1:T(8,128)(2,1)S(1)}, u32[]{:S(2)}, u32[]{:S(2)}) %collective-permute-start) | collective-permute-done | bytes 917536 | tf_op jit(solution)/shard_map/while/body/eval_jaxpr/ppermute | solution.py:14
  340.5 4.1 fusion.43
  347.8 3.9 multiply_add_fusion.5
  353.9 16.4 %collective-permute-done = bf16[896,512]{0,1:T(8,128)(2,1)S(1)} collective-permute-done((bf16[896,512]{0,1:T(8,128)(2,1)}, bf16[896,512]{0,1:T(8,128)(2,1)S(1)}, u32[]{:S(2)}, u32[]{:S(2)}) %collective-permute-start) | collective-permute-done | bytes 917536 | tf_op jit(solution)/shard_map/while/body/eval_jaxpr/ppermute | solution.py:14
  372.8 4.1 fusion.43
  380.1 3.9 multiply_add_fusion.5
  386.2 16.4 %collective-permute-done = bf16[896,512]{0,1:T(8,128)(2,1)S(1)} collective-permute-done((bf16[896,512]{0,1:T(8,128)(2,1)}, bf16[896,512]{0,1:T(8,128)(2,1)S(1)}, u32[]{:S(2)}, u32[]{:S(2)}) %collective-permute-start) | collective-permute-done | bytes 917536 | tf_op jit(solution)/shard_map/while/body/eval_jaxpr/ppermute | solution.py:14
  405.1 4.1 fusion.43
  412.4 3.9 multiply_add_fusion.5
  418.4 16.4 %collective-permute-done = bf16[896,512]{0,1:T(8,128)(2,1)S(1)} collective-permute-done((bf16[896,512]{0,1:T(8,128)(2,1)}, bf16[896,512]{0,1:T(8,128)(2,1)S(1)}, u32[]{:S(2)}, u32[]{:S(2)}) %collective-permute-start) | collective-permute-done | bytes 917536 | tf_op jit(solution)/shard_map/while/body/eval_jaxpr/ppermute | solution.py:14
  437.3 4.1 fusion.43
  450.7 16.4 %collective-permute-done = bf16[896,512]{0,1:T(8,128)(2,1)S(1)} collective-permute-done((bf16[896,512]{0,1:T(8,128)(2,1)}, bf16[896,512]{0,1:T(8,128)(2,1)S(1)}, u32[]{:S(2)}, u32[]{:S(2)}) %collective-permute-start) | collective-permute-done | bytes 917536 | tf_op jit(solution)/shard_map/while/body/eval_jaxpr/ppermute | solution.py:14
  469.6 4.1 fusion.43
  483.0 16.4 %collective-permute-done = bf16[896,512]{0,1:T(8,128)(2,1)S(1)} collective-permute-done((bf16[896,512]{0,1:T(8,128)(2,1)}, bf16[896,512]{0,1:T(8,128)(2,1)S(1)}, u32[]{:S(2)}, u32[]{:S(2)}) %collective-permute-start) | collective-permute-done | bytes 917536 | tf_op jit(solution)/shard_map/while/body/eval_jaxpr/ppermute | solution.py:14
  501.9 4.1 fusion.43
  515.3 16.4 %collective-permute-done = bf16[896,512]{0,1:T(8,128)(2,1)S(1)} collective-permute-done((bf16[896,512]{0,1:T(8,128)(2,1)}, bf16[896,512]{0,1:T(8,128)(2,1)S(1)}, u32[]{:S(2)}, u32[]{:S(2)}) %collective-permute-start) | collective-permute-done | bytes 917536 | tf_op jit(solution)/shard_map/while/body/eval_jaxpr/ppermute | solution.py:14
  534.2 4.1 fusion.43
  541.5 3.9 multiply_add_fusion.5
  547.5 16.4 %collective-permute-done = bf16[896,512]{0,1:T(8,128)(2,1)S(1)} collective-permute-done((bf16[896,512]{0,1:T(8,128)(2,1)}, bf16[896,512]{0,1:T(8,128)(2,1)S(1)}, u32[]{:S(2)}, u32[]{:S(2)}) %collective-permute-start) | collective-permute-done | bytes 917536 | tf_op jit(solution)/shard_map/while/body/eval_jaxpr/ppermute | solution.py:14
  566.4 4.1 fusion.43
  579.8 16.4 %collective-permute-done = bf16[896,512]{0,1:T(8,128)(2,1)S(1)} collective-permute-done((bf16[896,512]{0,1:T(8,128)(2,1)}, bf16[896,512]{0,1:T(8,128)(2,1)S(1)}, u32[]{:S(2)}, u32[]{:S(2)}) %collective-permute-start) | collective-permute-done | bytes 917536 | tf_op jit(solution)/shard_map/while/body/eval_jaxpr/ppermute | solution.py:14
  598.7 4.1 fusion.43
  612.1 16.4 %collective-permute-done = bf16[896,512]{0,1:T(8,128)(2,1)S(1)} collective-permute-done((bf16[896,512]{0,1:T(8,128)(2,1)}, bf16[896,512]{0,1:T(8,128)(2,1)S(1)}, u32[]{:S(2)}, u32[]{:S(2)}) %collective-permute-start) | collective-permute-done | bytes 917536 | tf_op jit(solution)/shard_map/while/body/eval_jaxpr/ppermute | solution.py:14
  631.0 4.1 fusion.43
  638.3 3.9 multiply_add_fusion.5
  (248 shorter events, 148.9 us)
Async XLA Ops:
  104.7 12.8 %copy-start.3 = (bf16[112,512]{1,0:T(8,128)(2,1)S(1)}, bf16[112,512]{1,0:T(8,128)(2,1)}, u32[]{:S(2)}) copy-start(bf16[112,512]{1,0:T(8,128)(2,1)} %param.8) | copy-start | bytes 344068
  108.8 4.6 copy-start
  150.0 9.8 %copy-start.4 = (s32[112]{0:T(128)S(1)}, s32[112]{0:T(128)}, u32[]{:S(2)}) copy-start(s32[112]{0:T(128)} %param.9) | copy-start | bytes 1348
  159.9 16.7 %collective-permute-start = (bf16[896,512]{0,1:T(8,128)(2,1)}, bf16[896,512]{0,1:T(8,128)(2,1)S(1)}, u32[]{:S(2)}, u32[]{:S(2)}) collective-permute-start(bf16[896,512]{0,1:T(8,128)(2,1)} %get-tuple-element.388), channel_id=1, source_target_pairs={{0,8},{8,16},{16,24},{24,32},{32,40},{40,48},{48,56},{56,64},{64,7... | collective-permute-start | bytes 2752520 | tf_op jit(solution)/shard_map/while/body/eval_jaxpr/ppermute | solution.py:14
  160.0 26.5 %collective-permute-start.1 = (bf16[896,512]{0,1:T(8,128)(2,1)}, bf16[896,512]{0,1:T(8,128)(2,1)S(1)}, u32[]{:S(2)}, u32[]{:S(2)}) collective-permute-start(bf16[896,512]{0,1:T(8,128)(2,1)} %get-tuple-element.389), channel_id=1, source_target_pairs={{0,8},{8,16},{16,24},{24,32},{32,40},{40,48},{48,56},{56,64},{64,7... | collective-permute-start | bytes 2752520 | tf_op jit(solution)/shard_map/while/body/eval_jaxpr/ppermute | solution.py:14
  176.6 9.8 %copy-start.1 = (f32[4,8,112,128]{3,2,1,0:T(8,128)S(1)}, f32[4,8,112,128]{3,2,1,0:T(8,128)}, u32[]{:S(2)}) copy-start(f32[4,8,112,128]{3,2,1,0:T(8,128)} %get-tuple-element.387) | copy-start | bytes 5505028 | tf_op jit(solution)/shard_map/while
  192.2 16.6 %collective-permute-start = (bf16[896,512]{0,1:T(8,128)(2,1)}, bf16[896,512]{0,1:T(8,128)(2,1)S(1)}, u32[]{:S(2)}, u32[]{:S(2)}) collective-permute-start(bf16[896,512]{0,1:T(8,128)(2,1)} %get-tuple-element.388), channel_id=1, source_target_pairs={{0,8},{8,16},{16,24},{24,32},{32,40},{40,48},{48,56},{56,64},{64,7... | collective-permute-start | bytes 2752520 | tf_op jit(solution)/shard_map/while/body/eval_jaxpr/ppermute | solution.py:14
  192.2 26.5 %collective-permute-start.1 = (bf16[896,512]{0,1:T(8,128)(2,1)}, bf16[896,512]{0,1:T(8,128)(2,1)S(1)}, u32[]{:S(2)}, u32[]{:S(2)}) collective-permute-start(bf16[896,512]{0,1:T(8,128)(2,1)} %get-tuple-element.389), channel_id=1, source_target_pairs={{0,8},{8,16},{16,24},{24,32},{32,40},{40,48},{48,56},{56,64},{64,7... | collective-permute-start | bytes 2752520 | tf_op jit(solution)/shard_map/while/body/eval_jaxpr/ppermute | solution.py:14
  208.9 9.8 %copy-start.1 = (f32[4,8,112,128]{3,2,1,0:T(8,128)S(1)}, f32[4,8,112,128]{3,2,1,0:T(8,128)}, u32[]{:S(2)}) copy-start(f32[4,8,112,128]{3,2,1,0:T(8,128)} %get-tuple-element.387) | copy-start | bytes 5505028 | tf_op jit(solution)/shard_map/while
  224.5 16.6 %collective-permute-start = (bf16[896,512]{0,1:T(8,128)(2,1)}, bf16[896,512]{0,1:T(8,128)(2,1)S(1)}, u32[]{:S(2)}, u32[]{:S(2)}) collective-permute-start(bf16[896,512]{0,1:T(8,128)(2,1)} %get-tuple-element.388), channel_id=1, source_target_pairs={{0,8},{8,16},{16,24},{24,32},{32,40},{40,48},{48,56},{56,64},{64,7... | collective-permute-start | bytes 2752520 | tf_op jit(solution)/shard_map/while/body/eval_jaxpr/ppermute | solution.py:14
  224.5 26.5 %collective-permute-start.1 = (bf16[896,512]{0,1:T(8,128)(2,1)}, bf16[896,512]{0,1:T(8,128)(2,1)S(1)}, u32[]{:S(2)}, u32[]{:S(2)}) collective-permute-start(bf16[896,512]{0,1:T(8,128)(2,1)} %get-tuple-element.389), channel_id=1, source_target_pairs={{0,8},{8,16},{16,24},{24,32},{32,40},{40,48},{48,56},{56,64},{64,7... | collective-permute-start | bytes 2752520 | tf_op jit(solution)/shard_map/while/body/eval_jaxpr/ppermute | solution.py:14
  241.2 9.8 %copy-start.1 = (f32[4,8,112,128]{3,2,1,0:T(8,128)S(1)}, f32[4,8,112,128]{3,2,1,0:T(8,128)}, u32[]{:S(2)}) copy-start(f32[4,8,112,128]{3,2,1,0:T(8,128)} %get-tuple-element.387) | copy-start | bytes 5505028 | tf_op jit(solution)/shard_map/while
  256.8 16.6 %collective-permute-start = (bf16[896,512]{0,1:T(8,128)(2,1)}, bf16[896,512]{0,1:T(8,128)(2,1)S(1)}, u32[]{:S(2)}, u32[]{:S(2)}) collective-permute-start(bf16[896,512]{0,1:T(8,128)(2,1)} %get-tuple-element.388), channel_id=1, source_target_pairs={{0,8},{8,16},{16,24},{24,32},{32,40},{40,48},{48,56},{56,64},{64,7... | collective-permute-start | bytes 2752520 | tf_op jit(solution)/shard_map/while/body/eval_jaxpr/ppermute | solution.py:14
  256.8 26.5 %collective-permute-start.1 = (bf16[896,512]{0,1:T(8,128)(2,1)}, bf16[896,512]{0,1:T(8,128)(2,1)S(1)}, u32[]{:S(2)}, u32[]{:S(2)}) collective-permute-start(bf16[896,512]{0,1:T(8,128)(2,1)} %get-tuple-element.389), channel_id=1, source_target_pairs={{0,8},{8,16},{16,24},{24,32},{32,40},{40,48},{48,56},{56,64},{64,7... | collective-permute-start | bytes 2752520 | tf_op jit(solution)/shard_map/while/body/eval_jaxpr/ppermute | solution.py:14
  273.4 9.8 %copy-start.1 = (f32[4,8,112,128]{3,2,1,0:T(8,128)S(1)}, f32[4,8,112,128]{3,2,1,0:T(8,128)}, u32[]{:S(2)}) copy-start(f32[4,8,112,128]{3,2,1,0:T(8,128)} %get-tuple-element.387) | copy-start | bytes 5505028 | tf_op jit(solution)/shard_map/while
  289.1 16.6 %collective-permute-start = (bf16[896,512]{0,1:T(8,128)(2,1)}, bf16[896,512]{0,1:T(8,128)(2,1)S(1)}, u32[]{:S(2)}, u32[]{:S(2)}) collective-permute-start(bf16[896,512]{0,1:T(8,128)(2,1)} %get-tuple-element.388), channel_id=1, source_target_pairs={{0,8},{8,16},{16,24},{24,32},{32,40},{40,48},{48,56},{56,64},{64,7... | collective-permute-start | bytes 2752520 | tf_op jit(solution)/shard_map/while/body/eval_jaxpr/ppermute | solution.py:14
  289.1 26.5 %collective-permute-start.1 = (bf16[896,512]{0,1:T(8,128)(2,1)}, bf16[896,512]{0,1:T(8,128)(2,1)S(1)}, u32[]{:S(2)}, u32[]{:S(2)}) collective-permute-start(bf16[896,512]{0,1:T(8,128)(2,1)} %get-tuple-element.389), channel_id=1, source_target_pairs={{0,8},{8,16},{16,24},{24,32},{32,40},{40,48},{48,56},{56,64},{64,7... | collective-permute-start | bytes 2752520 | tf_op jit(solution)/shard_map/while/body/eval_jaxpr/ppermute | solution.py:14
  305.7 9.8 %copy-start.1 = (f32[4,8,112,128]{3,2,1,0:T(8,128)S(1)}, f32[4,8,112,128]{3,2,1,0:T(8,128)}, u32[]{:S(2)}) copy-start(f32[4,8,112,128]{3,2,1,0:T(8,128)} %get-tuple-element.387) | copy-start | bytes 5505028 | tf_op jit(solution)/shard_map/while
  321.3 16.6 %collective-permute-start = (bf16[896,512]{0,1:T(8,128)(2,1)}, bf16[896,512]{0,1:T(8,128)(2,1)S(1)}, u32[]{:S(2)}, u32[]{:S(2)}) collective-permute-start(bf16[896,512]{0,1:T(8,128)(2,1)} %get-tuple-element.388), channel_id=1, source_target_pairs={{0,8},{8,16},{16,24},{24,32},{32,40},{40,48},{48,56},{56,64},{64,7... | collective-permute-start | bytes 2752520 | tf_op jit(solution)/shard_map/while/body/eval_jaxpr/ppermute | solution.py:14
  321.4 26.5 %collective-permute-start.1 = (bf16[896,512]{0,1:T(8,128)(2,1)}, bf16[896,512]{0,1:T(8,128)(2,1)S(1)}, u32[]{:S(2)}, u32[]{:S(2)}) collective-permute-start(bf16[896,512]{0,1:T(8,128)(2,1)} %get-tuple-element.389), channel_id=1, source_target_pairs={{0,8},{8,16},{16,24},{24,32},{32,40},{40,48},{48,56},{56,64},{64,7... | collective-permute-start | bytes 2752520 | tf_op jit(solution)/shard_map/while/body/eval_jaxpr/ppermute | solution.py:14
  338.0 9.8 %copy-start.1 = (f32[4,8,112,128]{3,2,1,0:T(8,128)S(1)}, f32[4,8,112,128]{3,2,1,0:T(8,128)}, u32[]{:S(2)}) copy-start(f32[4,8,112,128]{3,2,1,0:T(8,128)} %get-tuple-element.387) | copy-start | bytes 5505028 | tf_op jit(solution)/shard_map/while
  353.6 16.6 %collective-permute-start = (bf16[896,512]{0,1:T(8,128)(2,1)}, bf16[896,512]{0,1:T(8,128)(2,1)S(1)}, u32[]{:S(2)}, u32[]{:S(2)}) collective-permute-start(bf16[896,512]{0,1:T(8,128)(2,1)} %get-tuple-element.388), channel_id=1, source_target_pairs={{0,8},{8,16},{16,24},{24,32},{32,40},{40,48},{48,56},{56,64},{64,7... | collective-permute-start | bytes 2752520 | tf_op jit(solution)/shard_map/while/body/eval_jaxpr/ppermute | solution.py:14
  353.6 26.5 %collective-permute-start.1 = (bf16[896,512]{0,1:T(8,128)(2,1)}, bf16[896,512]{0,1:T(8,128)(2,1)S(1)}, u32[]{:S(2)}, u32[]{:S(2)}) collective-permute-start(bf16[896,512]{0,1:T(8,128)(2,1)} %get-tuple-element.389), channel_id=1, source_target_pairs={{0,8},{8,16},{16,24},{24,32},{32,40},{40,48},{48,56},{56,64},{64,7... | collective-permute-start | bytes 2752520 | tf_op jit(solution)/shard_map/while/body/eval_jaxpr/ppermute | solution.py:14
  370.3 9.8 %copy-start.1 = (f32[4,8,112,128]{3,2,1,0:T(8,128)S(1)}, f32[4,8,112,128]{3,2,1,0:T(8,128)}, u32[]{:S(2)}) copy-start(f32[4,8,112,128]{3,2,1,0:T(8,128)} %get-tuple-element.387) | copy-start | bytes 5505028 | tf_op jit(solution)/shard_map/while
  385.9 16.6 %collective-permute-start = (bf16[896,512]{0,1:T(8,128)(2,1)}, bf16[896,512]{0,1:T(8,128)(2,1)S(1)}, u32[]{:S(2)}, u32[]{:S(2)}) collective-permute-start(bf16[896,512]{0,1:T(8,128)(2,1)} %get-tuple-element.388), channel_id=1, source_target_pairs={{0,8},{8,16},{16,24},{24,32},{32,40},{40,48},{48,56},{56,64},{64,7... | collective-permute-start | bytes 2752520 | tf_op jit(solution)/shard_map/while/body/eval_jaxpr/ppermute | solution.py:14
  385.9 26.5 %collective-permute-start.1 = (bf16[896,512]{0,1:T(8,128)(2,1)}, bf16[896,512]{0,1:T(8,128)(2,1)S(1)}, u32[]{:S(2)}, u32[]{:S(2)}) collective-permute-start(bf16[896,512]{0,1:T(8,128)(2,1)} %get-tuple-element.389), channel_id=1, source_target_pairs={{0,8},{8,16},{16,24},{24,32},{32,40},{40,48},{48,56},{56,64},{64,7... | collective-permute-start | bytes 2752520 | tf_op jit(solution)/shard_map/while/body/eval_jaxpr/ppermute | solution.py:14
  402.5 9.8 %copy-start.1 = (f32[4,8,112,128]{3,2,1,0:T(8,128)S(1)}, f32[4,8,112,128]{3,2,1,0:T(8,128)}, u32[]{:S(2)}) copy-start(f32[4,8,112,128]{3,2,1,0:T(8,128)} %get-tuple-element.387) | copy-start | bytes 5505028 | tf_op jit(solution)/shard_map/while
  418.2 16.6 %collective-permute-start = (bf16[896,512]{0,1:T(8,128)(2,1)}, bf16[896,512]{0,1:T(8,128)(2,1)S(1)}, u32[]{:S(2)}, u32[]{:S(2)}) collective-permute-start(bf16[896,512]{0,1:T(8,128)(2,1)} %get-tuple-element.388), channel_id=1, source_target_pairs={{0,8},{8,16},{16,24},{24,32},{32,40},{40,48},{48,56},{56,64},{64,7... | collective-permute-start | bytes 2752520 | tf_op jit(solution)/shard_map/while/body/eval_jaxpr/ppermute | solution.py:14
  418.2 26.5 %collective-permute-start.1 = (bf16[896,512]{0,1:T(8,128)(2,1)}, bf16[896,512]{0,1:T(8,128)(2,1)S(1)}, u32[]{:S(2)}, u32[]{:S(2)}) collective-permute-start(bf16[896,512]{0,1:T(8,128)(2,1)} %get-tuple-element.389), channel_id=1, source_target_pairs={{0,8},{8,16},{16,24},{24,32},{32,40},{40,48},{48,56},{56,64},{64,7... | collective-permute-start | bytes 2752520 | tf_op jit(solution)/shard_map/while/body/eval_jaxpr/ppermute | solution.py:14
  434.8 9.8 %copy-start.1 = (f32[4,8,112,128]{3,2,1,0:T(8,128)S(1)}, f32[4,8,112,128]{3,2,1,0:T(8,128)}, u32[]{:S(2)}) copy-start(f32[4,8,112,128]{3,2,1,0:T(8,128)} %get-tuple-element.387) | copy-start | bytes 5505028 | tf_op jit(solution)/shard_map/while
  450.5 16.6 %collective-permute-start = (bf16[896,512]{0,1:T(8,128)(2,1)}, bf16[896,512]{0,1:T(8,128)(2,1)S(1)}, u32[]{:S(2)}, u32[]{:S(2)}) collective-permute-start(bf16[896,512]{0,1:T(8,128)(2,1)} %get-tuple-element.388), channel_id=1, source_target_pairs={{0,8},{8,16},{16,24},{24,32},{32,40},{40,48},{48,56},{56,64},{64,7... | collective-permute-start | bytes 2752520 | tf_op jit(solution)/shard_map/while/body/eval_jaxpr/ppermute | solution.py:14
  450.5 26.5 %collective-permute-start.1 = (bf16[896,512]{0,1:T(8,128)(2,1)}, bf16[896,512]{0,1:T(8,128)(2,1)S(1)}, u32[]{:S(2)}, u32[]{:S(2)}) collective-permute-start(bf16[896,512]{0,1:T(8,128)(2,1)} %get-tuple-element.389), channel_id=1, source_target_pairs={{0,8},{8,16},{16,24},{24,32},{32,40},{40,48},{48,56},{56,64},{64,7... | collective-permute-start | bytes 2752520 | tf_op jit(solution)/shard_map/while/body/eval_jaxpr/ppermute | solution.py:14
  467.1 9.8 %copy-start.1 = (f32[4,8,112,128]{3,2,1,0:T(8,128)S(1)}, f32[4,8,112,128]{3,2,1,0:T(8,128)}, u32[]{:S(2)}) copy-start(f32[4,8,112,128]{3,2,1,0:T(8,128)} %get-tuple-element.387) | copy-start | bytes 5505028 | tf_op jit(solution)/shard_map/while
  482.7 16.6 %collective-permute-start = (bf16[896,512]{0,1:T(8,128)(2,1)}, bf16[896,512]{0,1:T(8,128)(2,1)S(1)}, u32[]{:S(2)}, u32[]{:S(2)}) collective-permute-start(bf16[896,512]{0,1:T(8,128)(2,1)} %get-tuple-element.388), channel_id=1, source_target_pairs={{0,8},{8,16},{16,24},{24,32},{32,40},{40,48},{48,56},{56,64},{64,7... | collective-permute-start | bytes 2752520 | tf_op jit(solution)/shard_map/while/body/eval_jaxpr/ppermute | solution.py:14
  482.7 26.5 %collective-permute-start.1 = (bf16[896,512]{0,1:T(8,128)(2,1)}, bf16[896,512]{0,1:T(8,128)(2,1)S(1)}, u32[]{:S(2)}, u32[]{:S(2)}) collective-permute-start(bf16[896,512]{0,1:T(8,128)(2,1)} %get-tuple-element.389), channel_id=1, source_target_pairs={{0,8},{8,16},{16,24},{24,32},{32,40},{40,48},{48,56},{56,64},{64,7... | collective-permute-start | bytes 2752520 | tf_op jit(solution)/shard_map/while/body/eval_jaxpr/ppermute | solution.py:14
  499.4 9.8 %copy-start.1 = (f32[4,8,112,128]{3,2,1,0:T(8,128)S(1)}, f32[4,8,112,128]{3,2,1,0:T(8,128)}, u32[]{:S(2)}) copy-start(f32[4,8,112,128]{3,2,1,0:T(8,128)} %get-tuple-element.387) | copy-start | bytes 5505028 | tf_op jit(solution)/shard_map/while
  515.0 16.6 %collective-permute-start = (bf16[896,512]{0,1:T(8,128)(2,1)}, bf16[896,512]{0,1:T(8,128)(2,1)S(1)}, u32[]{:S(2)}, u32[]{:S(2)}) collective-permute-start(bf16[896,512]{0,1:T(8,128)(2,1)} %get-tuple-element.388), channel_id=1, source_target_pairs={{0,8},{8,16},{16,24},{24,32},{32,40},{40,48},{48,56},{56,64},{64,7... | collective-permute-start | bytes 2752520 | tf_op jit(solution)/shard_map/while/body/eval_jaxpr/ppermute | solution.py:14
  515.0 26.5 %collective-permute-start.1 = (bf16[896,512]{0,1:T(8,128)(2,1)}, bf16[896,512]{0,1:T(8,128)(2,1)S(1)}, u32[]{:S(2)}, u32[]{:S(2)}) collective-permute-start(bf16[896,512]{0,1:T(8,128)(2,1)} %get-tuple-element.389), channel_id=1, source_target_pairs={{0,8},{8,16},{16,24},{24,32},{32,40},{40,48},{48,56},{56,64},{64,7... | collective-permute-start | bytes 2752520 | tf_op jit(solution)/shard_map/while/body/eval_jaxpr/ppermute | solution.py:14
  531.7 9.8 %copy-start.1 = (f32[4,8,112,128]{3,2,1,0:T(8,128)S(1)}, f32[4,8,112,128]{3,2,1,0:T(8,128)}, u32[]{:S(2)}) copy-start(f32[4,8,112,128]{3,2,1,0:T(8,128)} %get-tuple-element.387) | copy-start | bytes 5505028 | tf_op jit(solution)/shard_map/while
  547.3 16.6 %collective-permute-start = (bf16[896,512]{0,1:T(8,128)(2,1)}, bf16[896,512]{0,1:T(8,128)(2,1)S(1)}, u32[]{:S(2)}, u32[]{:S(2)}) collective-permute-start(bf16[896,512]{0,1:T(8,128)(2,1)} %get-tuple-element.388), channel_id=1, source_target_pairs={{0,8},{8,16},{16,24},{24,32},{32,40},{40,48},{48,56},{56,64},{64,7... | collective-permute-start | bytes 2752520 | tf_op jit(solution)/shard_map/while/body/eval_jaxpr/ppermute | solution.py:14
  547.3 26.5 %collective-permute-start.1 = (bf16[896,512]{0,1:T(8,128)(2,1)}, bf16[896,512]{0,1:T(8,128)(2,1)S(1)}, u32[]{:S(2)}, u32[]{:S(2)}) collective-permute-start(bf16[896,512]{0,1:T(8,128)(2,1)} %get-tuple-element.389), channel_id=1, source_target_pairs={{0,8},{8,16},{16,24},{24,32},{32,40},{40,48},{48,56},{56,64},{64,7... | collective-permute-start | bytes 2752520 | tf_op jit(solution)/shard_map/while/body/eval_jaxpr/ppermute | solution.py:14
  563.9 9.8 %copy-start.1 = (f32[4,8,112,128]{3,2,1,0:T(8,128)S(1)}, f32[4,8,112,128]{3,2,1,0:T(8,128)}, u32[]{:S(2)}) copy-start(f32[4,8,112,128]{3,2,1,0:T(8,128)} %get-tuple-element.387) | copy-start | bytes 5505028 | tf_op jit(solution)/shard_map/while
  579.6 16.6 %collective-permute-start = (bf16[896,512]{0,1:T(8,128)(2,1)}, bf16[896,512]{0,1:T(8,128)(2,1)S(1)}, u32[]{:S(2)}, u32[]{:S(2)}) collective-permute-start(bf16[896,512]{0,1:T(8,128)(2,1)} %get-tuple-element.388), channel_id=1, source_target_pairs={{0,8},{8,16},{16,24},{24,32},{32,40},{40,48},{48,56},{56,64},{64,7... | collective-permute-start | bytes 2752520 | tf_op jit(solution)/shard_map/while/body/eval_jaxpr/ppermute | solution.py:14
  579.6 26.5 %collective-permute-start.1 = (bf16[896,512]{0,1:T(8,128)(2,1)}, bf16[896,512]{0,1:T(8,128)(2,1)S(1)}, u32[]{:S(2)}, u32[]{:S(2)}) collective-permute-start(bf16[896,512]{0,1:T(8,128)(2,1)} %get-tuple-element.389), channel_id=1, source_target_pairs={{0,8},{8,16},{16,24},{24,32},{32,40},{40,48},{48,56},{56,64},{64,7... | collective-permute-start | bytes 2752520 | tf_op jit(solution)/shard_map/while/body/eval_jaxpr/ppermute | solution.py:14
  596.2 9.8 %copy-start.1 = (f32[4,8,112,128]{3,2,1,0:T(8,128)S(1)}, f32[4,8,112,128]{3,2,1,0:T(8,128)}, u32[]{:S(2)}) copy-start(f32[4,8,112,128]{3,2,1,0:T(8,128)} %get-tuple-element.387) | copy-start | bytes 5505028 | tf_op jit(solution)/shard_map/while
  611.8 16.6 %collective-permute-start = (bf16[896,512]{0,1:T(8,128)(2,1)}, bf16[896,512]{0,1:T(8,128)(2,1)S(1)}, u32[]{:S(2)}, u32[]{:S(2)}) collective-permute-start(bf16[896,512]{0,1:T(8,128)(2,1)} %get-tuple-element.388), channel_id=1, source_target_pairs={{0,8},{8,16},{16,24},{24,32},{32,40},{40,48},{48,56},{56,64},{64,7... | collective-permute-start | bytes 2752520 | tf_op jit(solution)/shard_map/while/body/eval_jaxpr/ppermute | solution.py:14
  611.9 26.5 %collective-permute-start.1 = (bf16[896,512]{0,1:T(8,128)(2,1)}, bf16[896,512]{0,1:T(8,128)(2,1)S(1)}, u32[]{:S(2)}, u32[]{:S(2)}) collective-permute-start(bf16[896,512]{0,1:T(8,128)(2,1)} %get-tuple-element.389), channel_id=1, source_target_pairs={{0,8},{8,16},{16,24},{24,32},{32,40},{40,48},{48,56},{56,64},{64,7... | collective-permute-start | bytes 2752520 | tf_op jit(solution)/shard_map/while/body/eval_jaxpr/ppermute | solution.py:14
  628.5 9.8 %copy-start.1 = (f32[4,8,112,128]{3,2,1,0:T(8,128)S(1)}, f32[4,8,112,128]{3,2,1,0:T(8,128)}, u32[]{:S(2)}) copy-start(f32[4,8,112,128]{3,2,1,0:T(8,128)} %get-tuple-element.387) | copy-start | bytes 5505028 | tf_op jit(solution)/shard_map/while
  (15 other events, 28.5 us)
where the time goes:
time: 648 us
  waiting for transfers between devices  291 us (45%)
  blocking collectives  132 us (20%)
  matrix products  109 us (17%)
  other arithmetic  70.5 us (11%)
  local copies, waits for them, and re-layouts  40.9 us (6%)
    ppermute x30, waiting for transfers between devices, passed_along(): lax.ppermute(array, axis, [(i, (i + by) % count) for i in range(count)])  291 us
    unnamed x1, blocking collectives  68.7 us
    dot_general x16, matrix products, tile_step(): jnp.einsum('hgqk,khd->hgqd', weights.astype(jnp.bfloat16), value_heads, p...  67.9 us
    reduce_sum x16, other arithmetic, tile_step(): new_total = running_total * rescale + jnp.sum(weights, axis=-1)  65.5 us
    dot_general x16, matrix products, tile_step(): jnp.einsum('qhgd,khd->hgqk', query_heads, key_heads, preferred_element_ty...  41.5 us
    all_gather x1, blocking collectives, on_device(): lax.all_gather(keys, 'inner', axis=0, tiled=True)  31.7 us
    all_gather x1, blocking collectives, on_device(): lax.all_gather(values, 'inner', axis=0, tiled=True)  31.2 us
    while x105, local copies, waits for them, and re-layouts  28.4 us
  transfers between devices with their start and end apart: 30, of which 30 were waited for; matrix products, arithmetic and copies ran while one was open for 16% of the time, Pallas kernels for 0%

commit v1 on v0

v1 whole, which is shorter than its diff:
```python
import functools
import jax
import jax.numpy as jnp
from jax import lax
from jax.experimental import pallas as pl
from jax.experimental.pallas import tpu as pltpu
from jax.sharding import PartitionSpec as P

HEADS = 32
KV_HEADS = 4
D = 128
SPAN = 56
SEQ = 14336
RUNS = SEQ // SPAN
ROWS = 112
PEERS = 16
MESH = pl.DeviceIdType.MESH
LOG2E = 1.4426950408889634
SCALE = D ** -0.5 * LOG2E
HBM = pl.ANY
KEY_TILE = 1024
CHUNK = 256
TILE_RUNS = 4
HEADS_HERE = 2
TILE_ROWS = TILE_RUNS * SPAN
M = HEADS_HERE * TILE_ROWS
GROUP_RUNS = 2 * PEERS
SAFE = 90.0


def coords():
    outer, inner = lax.axis_index("outer"), lax.axis_index("inner")
    y, xh, core = outer // 4, (outer // 2) % 2, outer % 2
    return xh * 2 + inner % 2, y, inner // 2, core


def at(x, y, z, core):
    return ((y * 4 + (x // 2) * 2 + core), z * 2 + x % 2)


def greet(devices):
    barrier = pltpu.get_barrier_semaphore()
    for device in devices:
        pl.semaphore_signal(barrier, inc=1, device_id=device, device_id_type=MESH)
    pl.semaphore_wait(barrier, len(devices))


def group_peers(x, y, z, core):
    peers = []
    for d in range(1, PEERS):
        zz = (z + d // 4) % 4
        xx = (x // 2) * 2 + (x % 2 + (d // 2) % 2) % 2
        cc = (core + d % 2) % 2
        peers.append((xx, y, zz, cc))
    return peers


def slot_of(x, z, core):
    return z * 4 + (x % 2) * 2 + core


def gather_kernel(q_ref, k_ref, v_ref, qg_ref, kg_ref, vg_ref,
                  q_send, q_recv, z_send, z_recv, l_sem,
                  a_send, a_recv, b_send, b_recv, s_send, s_recv):
    x, y, z, core = coords()
    xr, xl, xo = (x + 1) % 4, (x + 3) % 4, (x + 2) % 4
    yr, yl, yo = (y + 1) % 4, (y + 3) % 4, (y + 2) % 4
    peers = group_peers(x, y, z, core)
    far_x = (x // 2) * 2 + (x + 1) % 2
    other_x = jnp.where(far_x == xr, xl, xr)
    greet([at(*p) for p in peers]
          + [at(other_x, y, z, core), at(x, yr, z, core), at(x, yl, z, core)])

    sent = []

    def send(src, dst, ssem, rsem, to):
        c = pltpu.make_async_remote_copy(
            src_ref=src, dst_ref=dst, send_sem=ssem, recv_sem=rsem,
            device_id=at(*to), device_id_type=MESH)
        c.start()
        sent.append(c)
        return c

    arrays = ((k_ref, kg_ref), (v_ref, vg_ref))
    zc = []
    for d in range(1, 4):
        zz = (z + d) % 4
        for i, (src, dst) in enumerate(arrays):
            zc.append(send(src.at[:, pl.ds(pl.multiple_of(zz * D, D), D)],
                           dst.at[core, y, x, pl.ds(pl.multiple_of(z * ROWS, 16), ROWS), :],
                           z_send.at[i, d], z_recv.at[i, d], (x, y, zz, core)))
    lc = []
    for i, (src, dst) in enumerate(arrays):
        c = pltpu.make_async_copy(src.at[:, pl.ds(pl.multiple_of(z * D, D), D)],
                                  dst.at[core, y, x, pl.ds(pl.multiple_of(z * ROWS, 16), ROWS), :],
                                  l_sem.at[i])
        c.start()
        lc.append(c)
    me = slot_of(x, z, core)
    qc = []
    for d, p in zip(range(1, PEERS), peers):
        t = slot_of(p[0], p[2], p[3])
        qc.append(send(q_ref.at[:, pl.ds(pl.multiple_of(t * 256, 256), 256)],
                       qg_ref.at[me], q_send.at[d], q_recv.at[d], p))
    c = pltpu.make_async_copy(q_ref.at[:, pl.ds(pl.multiple_of(me * 256, 256), 256)],
                              qg_ref.at[me], l_sem.at[2])
    c.start()
    lc.append(c)
    for c in zc:
        c.wait_recv()
    for c in lc:
        c.wait()

    half = 2 * ROWS

    def block(i, bx, by, h=None):
        ref = arrays[i][1]
        if h is None:
            return ref.at[core, by, bx]
        return ref.at[core, by, bx, pl.ds(h * half, half), :]

    sibling = (x, y, z, 1 - core)
    ring = (((xl, y), (xr, y)), ((x, yl), (x, yr)))
    cross = (((x, yl), (x, yr)), ((xl, y), (xr, y)))

    def to(pos):
        return (pos[0], pos[1], z, core)

    def hand(i, n, bx, by):
        ref = block(i, bx, by)
        return send(ref, ref, s_send.at[i, n], s_recv.at[i, n], sibling)

    sib = []

    def first(i):
        ref = block(i, x, y)
        lo, hi = ring[i]
        up = send(ref, ref, a_send.at[i, 0], a_recv.at[i, 0], to(hi))
        dn = send(ref, ref, a_send.at[i, 1], a_recv.at[i, 1], to(lo))
        return up, dn

    def second(i, n, bx, by):
        ref = block(i, bx, by)
        lo, hi = cross[i]
        up = send(ref, ref, b_send.at[i, n, 0], b_recv.at[i, n, 0], to(hi))
        dn = send(ref, ref, b_send.at[i, n, 1], b_recv.at[i, n, 1], to(lo))
        sib.append(hand(i, 4 * n, bx, by))
        return up, dn

    def along(i, bx, by, n):
        if i == 0:
            return ((bx, by), (xl, by), (xr, by), (xo, by))[n]
        return ((bx, by), (bx, yl), (bx, yr), (bx, yo))[n]

    def across(i, bx, by, n):
        if i == 0:
            return ((bx, by), (bx, yl), (bx, yr), (bx, yo))[n]
        return ((bx, by), (xl, by), (xr, by), (xo, by))[n]

    a = [first(0), first(1)]
    b = [[second(0, 0, x, y)], [second(1, 0, x, y)]]
    fwd = [None, None]
    for i in range(2):
        up, dn = a[i]
        lo, hi = ring[i]
        up.wait_recv()
        bx, by = along(i, x, y, 1)
        f1 = send(block(i, bx, by, 0), block(i, bx, by, 0), a_send.at[i, 2], a_recv.at[i, 2], to(hi))
        dn.wait_recv()
        cx, cy = along(i, x, y, 2)
        f2 = send(block(i, cx, cy, 1), block(i, cx, cy, 1), a_send.at[i, 3], a_recv.at[i, 3], to(lo))
        fwd[i] = (f1, f2)
        b[i].append(second(i, 1, bx, by))
        b[i].append(second(i, 2, cx, cy))

    def relay(i, n):
        bx, by = along(i, x, y, n)
        up, dn = b[i][n]
        lo, hi = cross[i]
        up.wait_recv()
        ux, uy = across(i, bx, by, 1)
        f1 = send(block(i, ux, uy, 0), block(i, ux, uy, 0), b_send.at[i, n, 2], b_recv.at[i, n, 2], to(hi))
        sib.append(hand(i, 4 * n + 1, ux, uy))
        dn.wait_recv()
        wx, wy = across(i, bx, by, 2)
        f2 = send(block(i, wx, wy, 1), block(i, wx, wy, 1), b_send.at[i, n, 3], b_recv.at[i, n, 3], to(lo))
        sib.append(hand(i, 4 * n + 2, wx, wy))
        return f1, f2

    last = [[], []]
    for i in range(2):
        last[i].append(relay(i, 0))
    for i in range(2):
        for f in fwd[i]:
            f.wait_recv()
        bx, by = along(i, x, y, 3)
        b[i].append(second(i, 3, bx, by))
    for n in range(1, 4):
        for i in range(2):
            last[i].append(relay(i, n))
    for n in range(4):
        for i in range(2):
            for f in last[i][n]:
                f.wait_recv()
            bx, by = along(i, x, y, n)
            ox, oy = across(i, bx, by, 3)
            sib.append(hand(i, 4 * n + 3, ox, oy))
    for c in qc:
        c.wait_recv()
    for c in sib:
        c.wait_recv()
    for c in sent:
        c.wait_send()


def gather(q, k, v):
    dma = pltpu.SemaphoreType.DMA
    return pl.pallas_call(
        gather_kernel,
        out_shape=(
            jax.ShapeDtypeStruct((PEERS, ROWS, 256), jnp.bfloat16),
            jax.ShapeDtypeStruct((2, 4, 4, 4 * ROWS, D), jnp.bfloat16),
            jax.ShapeDtypeStruct((2, 4, 4, 4 * ROWS, D), jnp.bfloat16),
        ),
        in_specs=[pl.BlockSpec(memory_space=HBM)] * 3,
        out_specs=[pl.BlockSpec(memory_space=HBM)] * 3,
        scratch_shapes=[
            dma((PEERS,)), dma((PEERS,)), dma((2, 4)), dma((2, 4)), dma((3,)),
            dma((2, 4)), dma((2, 4)), dma((2, 4, 4)), dma((2, 4, 4)), dma((2, 16)), dma((2, 16)),
        ],
        compiler_params=pltpu.CompilerParams(collective_id=0, has_side_effects=True),
        name="gather",
    )(q, k, v)


def return_kernel(o_ref, out_ref, send_sem, recv_sem, l_sem):
    x, y, z, core = coords()
    peers = group_peers(x, y, z, core)
    greet([at(*p) for p in peers])
    me = slot_of(x, z, core)
    there = out_ref.at[:, pl.ds(pl.multiple_of(me * 256, 256), 256)]
    copies = []
    for d, p in zip(range(1, PEERS), peers):
        c = pltpu.make_async_remote_copy(
            src_ref=o_ref.at[slot_of(p[0], p[2], p[3])], dst_ref=there,
            send_sem=send_sem.at[d], recv_sem=recv_sem.at[d],
            device_id=at(*p), device_id_type=MESH)
        c.start()
        copies.append(c)
    own = pltpu.make_async_copy(o_ref.at[me], there, l_sem)
    own.start()
    own.wait()
    for c in copies:
        c.wait_recv()
    for c in copies:
        c.wait_send()


def give_back(o):
    dma = pltpu.SemaphoreType.DMA
    return pl.pallas_call(
        return_kernel,
        out_shape=jax.ShapeDtypeStruct((ROWS, HEADS * D), jnp.bfloat16),
        in_specs=[pl.BlockSpec(memory_space=HBM)],
        out_specs=pl.BlockSpec(memory_space=HBM),
        scratch_shapes=[dma((PEERS,)), dma((PEERS,)), dma],
        compiler_params=pltpu.CompilerParams(collective_id=1, has_side_effects=True),
        name="give_back",
    )(o)


def half_of(ref, loc):
    pair = ref[pl.ds(pl.multiple_of((loc // 2) * ROWS, 16), ROWS), :].astype(jnp.float32)
    return jnp.where(loc % 2 == 1, pair[SPAN:], pair[:SPAN])


def attend_kernel(key_at, run_at, run_pos, norms, q_hbm, k_hbm, v_hbm, o_ref,
                  q_raw, k_raw, v_raw, k_sorted, v_sorted, q_tile, rel, acc, tot, top, out32, sem):
    copies = [pltpu.make_async_copy(src, dst, sem.at[i]) for i, (src, dst) in
              enumerate(((k_hbm, k_raw), (v_hbm, v_raw), (q_hbm, q_raw)))]
    for c in copies:
        c.start()
    for c in copies:
        c.wait()

    @pl.loop(0, RUNS // 2)
    def _(j):
        rows = pl.ds(pl.multiple_of(j * ROWS, 16), ROWS)
        a, b = key_at[2 * j], key_at[2 * j + 1]
        k2 = jnp.concatenate([half_of(k_raw, a), half_of(k_raw, b)], axis=0).astype(jnp.bfloat16)
        k_sorted[rows, :D] = k2
        k_sorted[rows, D:] = k2
        v2 = jnp.concatenate([half_of(v_raw, a), half_of(v_raw, b)], axis=0).astype(jnp.bfloat16)
        v_sorted[rows, :] = v2

    def scores(off, width):
        return lax.dot_general(q_tile[...], k_sorted[pl.ds(pl.multiple_of(off, 128), width), :],
                               (((1,), (1,)), ((), ())), preferred_element_type=jnp.float32)

    def product(p, off, width):
        return jnp.dot(p, v_sorted[pl.ds(pl.multiple_of(off, 128), width), :],
                       preferred_element_type=jnp.float32)

    def seen(off):
        return rel[...] >= off

    def plain(j, masked):
        off = j * KEY_TILE
        parts, total = [], None
        for i in range(KEY_TILE // CHUNK):
            s = scores(off + i * CHUNK, CHUNK)
            for w in range(CHUNK // 128):
                p = jnp.exp2(s[:, w * 128:(w + 1) * 128])
                if masked:
                    p = jnp.where(seen(off + i * CHUNK + w * 128), p, 0.0)
                total = p if total is None else total + p
                parts.append(p.astype(jnp.bfloat16))
        acc[...] += product(jnp.concatenate(parts, axis=1), off, KEY_TILE)
        tot[...] += total

    def guarded(j):
        for i in range(KEY_TILE // CHUNK):
            off = j * KEY_TILE + i * CHUNK
            s = scores(off, CHUNK)
            cols, vis, best = [], [], top[...]
            for w in range(CHUNK // 128):
                see = seen(off + w * 128)
                col = jnp.where(see, s[:, w * 128:(w + 1) * 128], -1e30)
                cols.append(col)
                vis.append(see)
                best = jnp.maximum(best, jnp.max(col, axis=1, keepdims=True))
            fade = jnp.exp2(top[...] - best)
            top[...] = best
            total = tot[...] * fade
            parts = []
            for col, see in zip(cols, vis):
                p = jnp.where(see, jnp.exp2(col - best), 0.0)
                total = total + p
                parts.append(p.astype(jnp.bfloat16))
            tot[...] = total
            acc[...] = acc[...] * fade + product(jnp.concatenate(parts, axis=1), off, CHUNK)

    @pl.loop(0, GROUP_RUNS // TILE_RUNS)
    def _(t):
        scaled, places = [], []
        for r in range(TILE_RUNS):
            loc = run_at[t * TILE_RUNS + r]
            scaled.append(half_of(q_raw, loc) * SCALE)
            first = run_pos[t * TILE_RUNS + r] * SPAN
            places.append(lax.broadcasted_iota(jnp.int32, (SPAN, 128), 0)
                          - lax.broadcasted_iota(jnp.int32, (SPAN, 128), 1) + first)
        whole = jnp.concatenate(scaled, axis=0)
        norm = jnp.float32(0)
        for h in range(HEADS_HERE):
            x = whole[:, h * D:(h + 1) * D]
            hi = x.astype(jnp.bfloat16)
            q_tile[h * TILE_ROWS:(h + 1) * TILE_ROWS, :D] = hi
            q_tile[h * TILE_ROWS:(h + 1) * TILE_ROWS, D:] = (x - hi.astype(jnp.float32)).astype(jnp.bfloat16)
            rel[h * TILE_ROWS:(h + 1) * TILE_ROWS, :] = jnp.concatenate(places, axis=0)
            norm = jnp.maximum(norm, jnp.max(jnp.sum(x * x, axis=1, keepdims=True)))
        acc[...] = jnp.zeros_like(acc)
        tot[...] = jnp.zeros_like(tot)
        low = run_pos[t * TILE_RUNS] * SPAN
        high = run_pos[t * TILE_RUNS + TILE_RUNS - 1] * SPAN + SPAN
        full = (low + 1) // KEY_TILE
        count = (high + KEY_TILE - 1) // KEY_TILE
        safe = norm * norms[0] < SAFE * SAFE

        @pl.when(safe)
        def _():
            @pl.loop(0, full)
            def _(j):
                plain(j, False)

            @pl.loop(full, count)
            def _(j):
                plain(j, True)

        @pl.when(jnp.logical_not(safe))
        def _():
            top[...] = jnp.full_like(top, -1e30)

            @pl.loop(0, count)
            def _(j):
                guarded(j)

        done = acc[...] / jnp.sum(tot[...], axis=1, keepdims=True)
        for r in range(TILE_RUNS):
            rows = pl.ds(pl.multiple_of(run_at[t * TILE_RUNS + r] * SPAN, 8), SPAN)
            for h in range(HEADS_HERE):
                out32[rows, h * D:(h + 1) * D] = done[h * TILE_ROWS + r * SPAN:h * TILE_ROWS + (r + 1) * SPAN]

    o_ref[...] = out32[...].astype(jnp.bfloat16)


def attend(key_at, run_at, run_pos, norms, q, k, v):
    smem = pl.BlockSpec(memory_space=pltpu.SMEM)
    rows = PEERS * ROWS
    return pl.pallas_call(
        attend_kernel,
        out_shape=jax.ShapeDtypeStruct((rows, 256), jnp.bfloat16),
        in_specs=[smem] * 4 + [pl.BlockSpec(memory_space=HBM)] * 3,
        out_specs=pl.BlockSpec(memory_space=pltpu.VMEM),
        scratch_shapes=[
            pltpu.VMEM((rows, 256), jnp.bfloat16),
            pltpu.VMEM((SEQ, D), jnp.bfloat16),
            pltpu.VMEM((SEQ, D), jnp.bfloat16),
            pltpu.VMEM((SEQ, 2 * D), jnp.bfloat16),
            pltpu.VMEM((SEQ, D), jnp.bfloat16),
            pltpu.VMEM((M, 2 * D), jnp.bfloat16),
            pltpu.VMEM((M, 128), jnp.int32),
            pltpu.VMEM((M, D), jnp.float32),
            pltpu.VMEM((M, 128), jnp.float32),
            pltpu.VMEM((M, 128), jnp.float32),
            pltpu.VMEM((rows, 256), jnp.float32),
            pltpu.SemaphoreType.DMA((3,)),
        ],
        compiler_params=pltpu.CompilerParams(vmem_limit_bytes=56 << 20),
        name="attend",
    )(key_at, run_at, run_pos, norms, q, k, v)


def on_device(queries, keys, values, positions):
    x, y, z, core = coords()
    squares = jnp.sum(jnp.square(keys.astype(jnp.float32).reshape(ROWS, KV_HEADS, D)), axis=-1)
    news = jnp.concatenate([positions[::SPAN].astype(jnp.float32), jnp.max(squares, axis=0)])
    all_news = lax.all_gather(news, ("outer", "inner"), axis=0, tiled=False)
    qg, kg, vg = gather(queries, keys, values)
    run_index = (all_news[:, :2].astype(jnp.int32) // SPAN).reshape(4, 2, 2, 4, 2, 2)
    norm = jnp.max(lax.dynamic_index_in_dim(all_news[:, 2:], z, 1, keepdims=False))
    places = jnp.arange(RUNS, dtype=jnp.int32)
    at_key = run_index.transpose(2, 0, 1, 4, 3, 5).reshape(RUNS)
    key_at = jnp.sum(jnp.where(at_key[None, :] == places[:, None], places[None, :], 0), axis=1)
    mine = lax.dynamic_index_in_dim(run_index, y, 0, keepdims=False)
    mine = lax.dynamic_index_in_dim(mine, x // 2, 0, keepdims=False)
    mine = mine.transpose(1, 2, 0, 3).reshape(GROUP_RUNS)
    rank = jnp.sum((mine[None, :] < mine[:, None]).astype(jnp.int32), axis=1)
    few = jnp.arange(GROUP_RUNS, dtype=jnp.int32)
    chosen = rank[None, :] == few[:, None]
    run_at = jnp.sum(jnp.where(chosen, few[None, :], 0), axis=1)
    run_pos = jnp.sum(jnp.where(chosen, mine[None, :], 0), axis=1)
    o = attend(key_at, run_at, run_pos, norm.reshape(1),
               qg.reshape(PEERS * ROWS, 256), kg.reshape(SEQ, D), vg.reshape(SEQ, D))
    return give_back(o.reshape(PEERS, ROWS, 256))


def solution(mesh):
    return jax.shard_map(
        on_device,
        mesh=mesh,
        in_specs=(
            P(("outer", "inner"), None),
            P(("outer", "inner"), None),
            P(("outer", "inner"), None),
            P(("outer", "inner")),
        ),
        out_specs=P(("outer", "inner"), None),
        check_vma=False,
    )
```

time: 648 us -> 229 us (0.35)
  the two profiles are of different devices: /device:TPU:0 before, /device:TPU:9 now
where the time goes in v1:
time: 229 us; the launch traced here: 227 us
  Pallas kernels  153 us (67%)
  blocking collectives  66.4 us (29%)
  local copies, waits for them, and re-layouts  4.3 us (2%)
  other arithmetic  3.68 us (2%)
    pallas_call x1, Pallas kernels, attend(): pl.pallas_call(attend_kernel, out_shape=jax.ShapeDtypeStruct((rows, 256),...  97.5 us
    unnamed x1, blocking collectives  66.4 us
    pallas_call x1, Pallas kernels, gather(): pl.pallas_call(gather_kernel, out_shape=(jax.ShapeDtypeStruct((PEERS, ROW...  39.7 us
    pallas_call x1, Pallas kernels, give_back(): pl.pallas_call(return_kernel, out_shape=jax.ShapeDtypeStruct((ROWS, HEADS...  15.4 us

profile of v1, /device:TPU:9, one launch (start us, length us, event | category | flops | bytes accessed | tf_op | source)
XLA Modules:
  0.0 227.1 jit_solution(13994963382460062604)
XLA Ops:
  0.0 0.7 slice.9
  0.7 0.9 convert_multiply_fusion
  1.7 0.1 square.7
  1.8 0.2 reduce_sum.45
  2.0 0.2 maximum_dynamic-update-slice_fusion
  2.2 66.4 %all-reduce = f32[768]{0:T(1024)S(1)} all-reduce(f32[768]{0:T(1024)S(1)} %maximum_dynamic-update-slice_fusion), channel_id=2, replica_groups=mesh['outer'=16,'inner'=8] {'outer','inner'}, use_global_device_ids=true, to_apply=%add | all-reduce | flops 768 | bytes 6144
  68.6 0.1 reshape.32
  68.7 0.1 copy.26
  68.8 0.2 reshape.26
  69.0 0.1 copy.24
  69.1 0.1 lt.41
  69.2 0.2 convert_reduce_fusion
  69.4 0.7 select_reduce_fusion.1
  70.1 0.5 copy.21
  70.6 0.1 eq.31
  70.8 0.7 select_reduce_fusion.key_at
  71.5 0.1 slice.13
  71.5 0.7 dynamic-slice_reduce_fusion
  72.3 39.7 %gather.1 = (bf16[16,112,256]{2,1,0:T(8,128)(2,1)}, bf16[2,4,4,448,128]{4,3,2,1,0:T(8,128)(2,1)}, bf16[2,4,4,448,128]{4,3,2,1,0:T(8,128)(2,1)}) custom-call(bf16[112,4096]{1,0:T(8,128)(2,1)} %q_ref.1, bf16[112,512]{1,0:T(8,128)(2,1)} %k_ref.1, bf16[112,512]{1,0:T(8,128)(2,1)} %v_ref.1), custom_call_target="tpu_custom_call" | custom-call | tf_op jit(solution)/shard_map/gather/pallas_call | solution.py:218
  112.0 97.5 %attend.1 = bf16[1792,256]{1,0:T(8,128)(2,1)} custom-call(s32[256]{0:T(256)} %select_reduce_fusion.key_at, s32[32]{0:T(128)} %get-tuple-element.12.run_at, s32[32]{0:T(128)} %get-tuple-element.11.run_pos, f32[1]{0:T(128)} %bitcast.4.norms, bf16[1792,256]{1,0:T(8,128)(2,1)} %bitcast.15, bf16[14336,128]{1,0:T(8,128)(2,1)} %bitcast.12, bf16[14336,128]{1,0:T(8,128)(2,1)} %bitcast.13), custom_call_target="tpu_custom_call" | custom-call | tf_op jit(solution)/shard_map/attend/pallas_call | solution.py:399
  209.5 15.4 %give_back.1 = bf16[112,4096]{1,0:T(8,128)(2,1)} custom-call(bf16[16,112,256]{2,1,0:T(8,128)(2,1)} %bitcast.14), custom_call_target="tpu_custom_call" | custom-call | tf_op jit(solution)/shard_map/give_back/pallas_call | solution.py:261
  224.9 2.2 copy.29
  (5 shorter events, 0.1 us)

commit v2 on v1

--- a/solution.py
+++ b/solution.py
@@ -13,12 +13,15 @@
 SEQ = 14336
 RUNS = SEQ // SPAN
 ROWS = 112
+KROWS = 128
 PEERS = 16
 MESH = pl.DeviceIdType.MESH
 LOG2E = 1.4426950408889634
 SCALE = D ** -0.5 * LOG2E
 HBM = pl.ANY
-KEY_TILE = 1024
+KEY_TILE = 2048
+PIECE = 512
+PREP = 8
 CHUNK = 256
 TILE_RUNS = 4
 HEADS_HERE = 2
@@ -59,7 +62,7 @@
     return z * 4 + (x % 2) * 2 + core
 
 
-def gather_kernel(q_ref, k_ref, v_ref, qg_ref, kg_ref, vg_ref,
+def gather_kernel(q_ref, k_ref, v_ref, news_ref, qg_ref, kg_ref, vg_ref,
                   q_send, q_recv, z_send, z_recv, l_sem,
                   a_send, a_recv, b_send, b_recv, s_send, s_recv):
     x, y, z, core = coords()
@@ -82,18 +85,22 @@
         return c
 
     arrays = ((k_ref, kg_ref), (v_ref, vg_ref))
-    zc = []
+    deep = (KROWS, ROWS)
+    def slot(i, rows, start=0):
+        return arrays[i][1].at[core, y, x, pl.ds(pl.multiple_of(z * deep[i] + start, 16), rows), :]
+
+    def columns(i, head):
+        return arrays[i][0].at[:, pl.ds(pl.multiple_of(head * D, D), D)]
+
+    zc, lc = [], []
     for d in range(1, 4):
         zz = (z + d) % 4
-        for i, (src, dst) in enumerate(arrays):
-            zc.append(send(src.at[:, pl.ds(pl.multiple_of(zz * D, D), D)],
-                           dst.at[core, y, x, pl.ds(pl.multiple_of(z * ROWS, 16), ROWS), :],
-                           z_send.at[i, d], z_recv.at[i, d], (x, y, zz, core)))
-    lc = []
-    for i, (src, dst) in enumerate(arrays):
-        c = pltpu.make_async_copy(src.at[:, pl.ds(pl.multiple_of(z * D, D), D)],
-                                  dst.at[core, y, x, pl.ds(pl.multiple_of(z * ROWS, 16), ROWS), :],
-                                  l_sem.at[i])
+        for i in range(2):
+            zc.append(send(columns(i, zz), slot(i, ROWS), z_send.at[i, d], z_recv.at[i, d], (x, y, zz, core)))
+        zc.append(send(news_ref, slot(0, KROWS - ROWS, ROWS), z_send.at[2, d], z_recv.at[2, d], (x, y, zz, core)))
+    for i, (src, dst) in enumerate(((columns(0, z), slot(0, ROWS)), (columns(1, z), slot(1, ROWS)),
+                                    (news_ref, slot(0, KROWS - ROWS, ROWS)))):
+        c = pltpu.make_async_copy(src, dst, l_sem.at[i])
         c.start()
         lc.append(c)
     me = slot_of(x, z, core)
@@ -103,7 +110,7 @@
         qc.append(send(q_ref.at[:, pl.ds(pl.multiple_of(t * 256, 256), 256)],
                        qg_ref.at[me], q_send.at[d], q_recv.at[d], p))
     c = pltpu.make_async_copy(q_ref.at[:, pl.ds(pl.multiple_of(me * 256, 256), 256)],
-                              qg_ref.at[me], l_sem.at[2])
+                              qg_ref.at[me], l_sem.at[3])
     c.start()
     lc.append(c)
     for c in zc:
@@ -111,10 +118,8 @@
     for c in lc:
         c.wait()
 
-    half = 2 * ROWS
-
     def block(i, bx, by, h=None):
-        ref = arrays[i][1]
+        ref, half = arrays[i][1], 2 * deep[i]
         if h is None:
             return ref.at[core, by, bx]
         return ref.at[core, by, bx, pl.ds(h * half, half), :]
@@ -213,24 +218,24 @@
         c.wait_send()
 
 
-def gather(q, k, v):
+def gather(q, k, v, news):
     dma = pltpu.SemaphoreType.DMA
     return pl.pallas_call(
         gather_kernel,
         out_shape=(
             jax.ShapeDtypeStruct((PEERS, ROWS, 256), jnp.bfloat16),
-            jax.ShapeDtypeStruct((2, 4, 4, 4 * ROWS, D), jnp.bfloat16),
+            jax.ShapeDtypeStruct((2, 4, 4, 4 * KROWS, D), jnp.bfloat16),
             jax.ShapeDtypeStruct((2, 4, 4, 4 * ROWS, D), jnp.bfloat16),
         ),
-        in_specs=[pl.BlockSpec(memory_space=HBM)] * 3,
+        in_specs=[pl.BlockSpec(memory_space=HBM)] * 4,
         out_specs=[pl.BlockSpec(memory_space=HBM)] * 3,
         scratch_shapes=[
-            dma((PEERS,)), dma((PEERS,)), dma((2, 4)), dma((2, 4)), dma((3,)),
+            dma((PEERS,)), dma((PEERS,)), dma((3, 4)), dma((3, 4)), dma((4,)),
             dma((2, 4)), dma((2, 4)), dma((2, 4, 4)), dma((2, 4, 4)), dma((2, 16)), dma((2, 16)),
         ],
         compiler_params=pltpu.CompilerParams(collective_id=0, has_side_effects=True),
         name="gather",
-    )(q, k, v)
+    )(q, k, v, news)
 
 
 def return_kernel(o_ref, out_ref, send_sem, recv_sem, l_sem):
@@ -269,45 +274,71 @@
     )(o)
 
 
-def half_of(ref, loc):
-    pair = ref[pl.ds(pl.multiple_of((loc // 2) * ROWS, 16), ROWS), :].astype(jnp.float32)
+def half_of(ref, loc, stride=ROWS):
+    pair = ref[pl.ds(pl.multiple_of((loc // 2) * stride, 16), ROWS), :].astype(jnp.float32)
     return jnp.where(loc % 2 == 1, pair[SPAN:], pair[:SPAN])
 
 
-def attend_kernel(key_at, run_at, run_pos, norms, q_hbm, k_hbm, v_hbm, o_ref,
-                  q_raw, k_raw, v_raw, k_sorted, v_sorted, q_tile, rel, acc, tot, top, out32, sem):
+def attend_kernel(run_index, spot, q_hbm, k_hbm, v_hbm, o_ref,
+                  q_raw, k_raw, v_raw, k_sorted, v_sorted, q_tile, rel, acc, tot, top, out32,
+                  key_at, own, run_at, run_pos, sem):
     copies = [pltpu.make_async_copy(src, dst, sem.at[i]) for i, (src, dst) in
               enumerate(((k_hbm, k_raw), (v_hbm, v_raw), (q_hbm, q_raw)))]
     for c in copies:
         c.start()
+
+    for p in range(RUNS):
+        own[p] = -1
+    for loc in range(RUNS):
+        key_at[run_index[loc]] = loc
+    for i in range(GROUP_RUNS):
+        z, x_lo, core, half = i // 8, (i // 4) % 2, (i // 2) % 2, i % 2
+        loc = (core * 4 + spot[0]) * 32 + (spot[1] * 2 + x_lo) * 8 + z * 2 + half
+        own[run_index[loc]] = i
+    n = jnp.int32(0)
+    for p in range(RUNS):
+        who = own[p]
+        run_at[n] = who
+        run_pos[n] = p
+        n = n + jnp.where(who >= 0, 1, 0)
     for c in copies:
         c.wait()
 
-    @pl.loop(0, RUNS // 2)
-    def _(j):
-        rows = pl.ds(pl.multiple_of(j * ROWS, 16), ROWS)
-        a, b = key_at[2 * j], key_at[2 * j + 1]
-        k2 = jnp.concatenate([half_of(k_raw, a), half_of(k_raw, b)], axis=0).astype(jnp.bfloat16)
-        k_sorted[rows, :D] = k2
-        k_sorted[rows, D:] = k2
-        v2 = jnp.concatenate([half_of(v_raw, a), half_of(v_raw, b)], axis=0).astype(jnp.bfloat16)
-        v_sorted[rows, :] = v2
+    @pl.loop(0, RUNS // 2 // PREP)
+    def _(step):
+        for i in range(PREP):
+            j = step * PREP + i
+            rows = pl.ds(pl.multiple_of(j * ROWS, 16), ROWS)
+            a, b = key_at[2 * j], key_at[2 * j + 1]
+            k2 = jnp.concatenate([half_of(k_raw, a, KROWS), half_of(k_raw, b, KROWS)], axis=0).astype(jnp.bfloat16)
+            k_sorted[rows, :] = k2
+            v2 = jnp.concatenate([half_of(v_raw, a), half_of(v_raw, b)], axis=0).astype(jnp.bfloat16)
+            v_sorted[rows, :] = v2
+
+    ones = jnp.ones((D, D), jnp.bfloat16)
+    longest = None
+    for i in range(SEQ // 2048):
+        keys = k_sorted[i * 2048:(i + 1) * 2048, :]
+        square = jnp.dot(keys * keys, ones, preferred_element_type=jnp.float32)
+        square = jnp.max(square, axis=0, keepdims=True)
+        longest = square if longest is None else jnp.maximum(longest, square)
+    key_norm = jnp.max(longest) * 1.01
 
     def scores(off, width):
         return lax.dot_general(q_tile[...], k_sorted[pl.ds(pl.multiple_of(off, 128), width), :],
-                               (((1,), (1,)), ((), ())), preferred_element_type=jnp.float32)
+                               (((1,), (1,)), ((), ())), preferred_element_type=jnp.float32) * SCALE
 
     def product(p, off, width):
         return jnp.dot(p, v_sorted[pl.ds(pl.multiple_of(off, 128), width), :],
                        preferred_element_type=jnp.float32)
 
     def seen(off):
-        return rel[...] >= off
-
-    def plain(j, masked):
-        off = j * KEY_TILE
+        see = rel[...] >= off
+        return jnp.concatenate([see] * HEADS_HERE, axis=0)
+
+    def plain(off, width, masked):
         parts, total = [], None
-        for i in range(KEY_TILE // CHUNK):
+        for i in range(width // CHUNK):
             s = scores(off + i * CHUNK, CHUNK)
             for w in range(CHUNK // 128):
                 p = jnp.exp2(s[:, w * 128:(w + 1) * 128])
@@ -315,37 +346,35 @@
                     p = jnp.where(seen(off + i * CHUNK + w * 128), p, 0.0)
                 total = p if total is None else total + p
                 parts.append(p.astype(jnp.bfloat16))
-        acc[...] += product(jnp.concatenate(parts, axis=1), off, KEY_TILE)
+        acc[...] += product(jnp.concatenate(parts, axis=1), off, width)
         tot[...] += total
 
-    def guarded(j):
-        for i in range(KEY_TILE // CHUNK):
-            off = j * KEY_TILE + i * CHUNK
-            s = scores(off, CHUNK)
-            cols, vis, best = [], [], top[...]
-            for w in range(CHUNK // 128):
-                see = seen(off + w * 128)
-                col = jnp.where(see, s[:, w * 128:(w + 1) * 128], -1e30)
-                cols.append(col)
-                vis.append(see)
-                best = jnp.maximum(best, jnp.max(col, axis=1, keepdims=True))
-            fade = jnp.exp2(top[...] - best)
-            top[...] = best
-            total = tot[...] * fade
-            parts = []
-            for col, see in zip(cols, vis):
-                p = jnp.where(see, jnp.exp2(col - best), 0.0)
-                total = total + p
-                parts.append(p.astype(jnp.bfloat16))
-            tot[...] = total
-            acc[...] = acc[...] * fade + product(jnp.concatenate(parts, axis=1), off, CHUNK)
+    def guarded(off):
+        s = scores(off, CHUNK)
+        cols, vis, best = [], [], top[...]
+        for w in range(CHUNK // 128):
+            see = seen(off + w * 128)
+            col = jnp.where(see, s[:, w * 128:(w + 1) * 128], -1e30)
+            cols.append(col)
+            vis.append(see)
+            best = jnp.maximum(best, jnp.max(col, axis=1, keepdims=True))
+        fade = jnp.exp2(top[...] - best)
+        top[...] = best
+        total = tot[...] * fade
+        parts = []
+        for col, see in zip(cols, vis):
+            p = jnp.where(see, jnp.exp2(col - best), 0.0)
+            total = total + p
+            parts.append(p.astype(jnp.bfloat16))
+        tot[...] = total
+        acc[...] = acc[...] * fade + product(jnp.concatenate(parts, axis=1), off, CHUNK)
 
     @pl.loop(0, GROUP_RUNS // TILE_RUNS)
     def _(t):
         scaled, places = [], []
         for r in range(TILE_RUNS):
             loc = run_at[t * TILE_RUNS + r]
-            scaled.append(half_of(q_raw, loc) * SCALE)
+            scaled.append(half_of(q_raw, loc))
             first = run_pos[t * TILE_RUNS + r] * SPAN
             places.append(lax.broadcasted_iota(jnp.int32, (SPAN, 128), 0)
                           - lax.broadcasted_iota(jnp.int32, (SPAN, 128), 1) + first)
@@ -353,36 +382,42 @@
         norm = jnp.float32(0)
         for h in range(HEADS_HERE):
             x = whole[:, h * D:(h + 1) * D]
-            hi = x.astype(jnp.bfloat16)
-            q_tile[h * TILE_ROWS:(h + 1) * TILE_ROWS, :D] = hi
-            q_tile[h * TILE_ROWS:(h + 1) * TILE_ROWS, D:] = (x - hi.astype(jnp.float32)).astype(jnp.bfloat16)
-            rel[h * TILE_ROWS:(h + 1) * TILE_ROWS, :] = jnp.concatenate(places, axis=0)
+            q_tile[h * TILE_ROWS:(h + 1) * TILE_ROWS, :] = x.astype(jnp.bfloat16)
             norm = jnp.maximum(norm, jnp.max(jnp.sum(x * x, axis=1, keepdims=True)))
+        rel[...] = jnp.concatenate(places, axis=0)
         acc[...] = jnp.zeros_like(acc)
         tot[...] = jnp.zeros_like(tot)
         low = run_pos[t * TILE_RUNS] * SPAN
         high = run_pos[t * TILE_RUNS + TILE_RUNS - 1] * SPAN + SPAN
         full = (low + 1) // KEY_TILE
-        count = (high + KEY_TILE - 1) // KEY_TILE
-        safe = norm * norms[0] < SAFE * SAFE
+        pieces = (high + PIECE - 1) // PIECE
+        many = KEY_TILE // PIECE
+        masked = full + jnp.maximum(pieces - full * many - many, 0) // many
+        left = pieces - masked * many
+        safe = norm * key_norm * (SCALE * SCALE) < SAFE * SAFE
 
         @pl.when(safe)
         def _():
             @pl.loop(0, full)
             def _(j):
-                plain(j, False)
-
-            @pl.loop(full, count)
+                plain(j * KEY_TILE, KEY_TILE, False)
+
+            @pl.loop(full, masked)
             def _(j):
-                plain(j, True)
+                plain(j * KEY_TILE, KEY_TILE, True)
+
+            for n in range(1, 2 * many):
+                @pl.when(left == n)
+                def _():
+                    plain(masked * KEY_TILE, n * PIECE, True)
 
         @pl.when(jnp.logical_not(safe))
         def _():
             top[...] = jnp.full_like(top, -1e30)
 
-            @pl.loop(0, count)
+            @pl.loop(0, (high + CHUNK - 1) // CHUNK)
             def _(j):
-                guarded(j)
+                guarded(j * CHUNK)
 
         done = acc[...] / jnp.sum(tot[...], axis=1, keepdims=True)
         for r in range(TILE_RUNS):
@@ -393,54 +428,46 @@
     o_ref[...] = out32[...].astype(jnp.bfloat16)
 
 
-def attend(key_at, run_at, run_pos, norms, q, k, v):
+def attend(run_index, spot, q, k, v):
     smem = pl.BlockSpec(memory_space=pltpu.SMEM)
     rows = PEERS * ROWS
     return pl.pallas_call(
         attend_kernel,
         out_shape=jax.ShapeDtypeStruct((rows, 256), jnp.bfloat16),
-        in_specs=[smem] * 4 + [pl.BlockSpec(memory_space=HBM)] * 3,
+        in_specs=[smem] * 2 + [pl.BlockSpec(memory_space=HBM)] * 3,
         out_specs=pl.BlockSpec(memory_space=pltpu.VMEM),
         scratch_shapes=[
             pltpu.VMEM((rows, 256), jnp.bfloat16),
+            pltpu.VMEM((RUNS // 2 * KROWS, D), jnp.bfloat16),
             pltpu.VMEM((SEQ, D), jnp.bfloat16),
             pltpu.VMEM((SEQ, D), jnp.bfloat16),
-            pltpu.VMEM((SEQ, 2 * D), jnp.bfloat16),
             pltpu.VMEM((SEQ, D), jnp.bfloat16),
-            pltpu.VMEM((M, 2 * D), jnp.bfloat16),
-            pltpu.VMEM((M, 128), jnp.int32),
+            pltpu.VMEM((M, D), jnp.bfloat16),
+            pltpu.VMEM((TILE_ROWS, 128), jnp.int32),
             pltpu.VMEM((M, D), jnp.float32),
             pltpu.VMEM((M, 128), jnp.float32),
             pltpu.VMEM((M, 128), jnp.float32),
             pltpu.VMEM((rows, 256), jnp.float32),
+            pltpu.SMEM((RUNS,), jnp.int32),
+            pltpu.SMEM((RUNS,), jnp.int32),
+            pltpu.SMEM((GROUP_RUNS + 1,), jnp.int32),
+            pltpu.SMEM((GROUP_RUNS + 1,), jnp.int32),
             pltpu.SemaphoreType.DMA((3,)),
         ],
         compiler_params=pltpu.CompilerParams(vmem_limit_bytes=56 << 20),
         name="attend",
-    )(key_at, run_at, run_pos, norms, q, k, v)
+    )(run_index, spot, q, k, v)
 
 
 def on_device(queries, keys, values, positions):
     x, y, z, core = coords()
-    squares = jnp.sum(jnp.square(keys.astype(jnp.float32).reshape(ROWS, KV_HEADS, D)), axis=-1)
-    news = jnp.concatenate([positions[::SPAN].astype(jnp.float32), jnp.max(squares, axis=0)])
-    all_news = lax.all_gather(news, ("outer", "inner"), axis=0, tiled=False)
-    qg, kg, vg = gather(queries, keys, values)
-    run_index = (all_news[:, :2].astype(jnp.int32) // SPAN).reshape(4, 2, 2, 4, 2, 2)
-    norm = jnp.max(lax.dynamic_index_in_dim(all_news[:, 2:], z, 1, keepdims=False))
-    places = jnp.arange(RUNS, dtype=jnp.int32)
-    at_key = run_index.transpose(2, 0, 1, 4, 3, 5).reshape(RUNS)
-    key_at = jnp.sum(jnp.where(at_key[None, :] == places[:, None], places[None, :], 0), axis=1)
-    mine = lax.dynamic_index_in_dim(run_index, y, 0, keepdims=False)
-    mine = lax.dynamic_index_in_dim(mine, x // 2, 0, keepdims=False)
-    mine = mine.transpose(1, 2, 0, 3).reshape(GROUP_RUNS)
-    rank = jnp.sum((mine[None, :] < mine[:, None]).astype(jnp.int32), axis=1)
-    few = jnp.arange(GROUP_RUNS, dtype=jnp.int32)
-    chosen = rank[None, :] == few[:, None]
-    run_at = jnp.sum(jnp.where(chosen, few[None, :], 0), axis=1)
-    run_pos = jnp.sum(jnp.where(chosen, mine[None, :], 0), axis=1)
-    o = attend(key_at, run_at, run_pos, norm.reshape(1),
-               qg.reshape(PEERS * ROWS, 256), kg.reshape(SEQ, D), vg.reshape(SEQ, D))
+    runs = (positions[::SPAN] // SPAN).astype(jnp.bfloat16)
+    news = jnp.broadcast_to(jnp.pad(runs, (0, D - 2)), (KROWS - ROWS, D))
+    qg, kg, vg = gather(queries, keys, values, news)
+    run_index = kg.reshape(RUNS // 2, KROWS, D)[:, ROWS, :2].astype(jnp.int32).reshape(RUNS)
+    spot = jnp.stack([y, x // 2]).astype(jnp.int32)
+    o = attend(run_index, spot, qg.reshape(PEERS * ROWS, 256),
+               kg.reshape(RUNS // 2 * KROWS, D), vg.reshape(SEQ, D))
     return give_back(o.reshape(PEERS, ROWS, 256))
 
 

time: 229 us -> 214 us (0.934)
  blocking collectives: 66.4 us -> 0 us
  Pallas kernels: 153 us -> 208 us
  other arithmetic: 3.68 us -> 0.68 us
    unnamed x1 -> x0, blocking collectives: 66.4 us -> none
    pallas_call x1, Pallas kernels: 97.5 us -> 148 us  [attend(): pl.pallas_call(attend_kernel, out_shape=jax.ShapeDtypeStruct((rows, 256),...]
    pallas_call x1, Pallas kernels: 39.7 us -> 44.5 us  [gather(): pl.pallas_call(gather_kernel, out_shape=(jax.ShapeDtypeStruct((PEERS, ROW...]
where the time goes in v2:
time: 214 us; the launch traced here: 213 us
  Pallas kernels  208 us (97%)
  local copies, waits for them, and re-layouts  5.17 us (2%)
    pallas_call x1, Pallas kernels, attend(): pl.pallas_call(attend_kernel, out_shape=jax.ShapeDtypeStruct((rows, 256),...  148 us
    pallas_call x1, Pallas kernels, gather(): pl.pallas_call(gather_kernel, out_shape=(jax.ShapeDtypeStruct((PEERS, ROW...  44.5 us
    pallas_call x1, Pallas kernels, give_back(): pl.pallas_call(return_kernel, out_shape=jax.ShapeDtypeStruct((ROWS, HEADS...  15 us

profile of v2, /device:TPU:9, one launch (start us, length us, event | category | flops | bytes accessed | tf_op | source)
XLA Modules:
  0.0 213.5 jit_solution(8392014396959337527)
XLA Ops:
  0.0 0.6 pad_add_fusion.spot
  0.6 0.7 slice.6
  1.4 0.6 broadcast_in_dim.3.news_ref
  2.0 44.5 %gather.1 = (bf16[16,112,256]{2,1,0:T(8,128)(2,1)}, bf16[2,4,4,512,128]{4,3,2,1,0:T(8,128)(2,1)}, bf16[2,4,4,448,128]{4,3,2,1,0:T(8,128)(2,1)}) custom-call(bf16[112,4096]{1,0:T(8,128)(2,1)} %q_ref.1, bf16[112,512]{1,0:T(8,128)(2,1)} %k_ref.1, bf16[112,512]{1,0:T(8,128)(2,1)} %v_ref.1, bf16[16,128]{1,0:T(8,128)(2,1)} %broadcast_in_dim.3.news_ref), custom_call_target="tpu_custom_call" | custom-call | tf_op jit(solution)/shard_map/gather/pallas_call | solution.py:223
  46.5 1.0 slice.8
  47.5 0.7 reshape.24.run_index
  48.2 148.1 %attend.1 = bf16[1792,256]{1,0:T(8,128)(2,1)} custom-call(s32[256]{0:T(256)} %reshape.24.run_index, s32[2]{0:T(128)} %pad_add_fusion.spot, bf16[1792,256]{1,0:T(8,128)(2,1)} %bitcast.13, bf16[16384,128]{1,0:T(8,128)(2,1)} %bitcast.10, bf16[14336,128]{1,0:T(8,128)(2,1)} %bitcast.12), custom_call_target="tpu_custom_call" | custom-call | tf_op jit(solution)/shard_map/attend/pallas_call | solution.py:434
  196.3 15.0 %give_back.1 = bf16[112,4096]{1,0:T(8,128)(2,1)} custom-call(bf16[16,112,256]{2,1,0:T(8,128)(2,1)} %bitcast.11), custom_call_target="tpu_custom_call" | custom-call | tf_op jit(solution)/shard_map/give_back/pallas_call | solution.py:266
  211.3 2.2 %copy.9 = bf16[112,4096]{1,0:T(8,128)(2,1)} copy(bf16[112,4096]{1,0:T(8,128)(2,1)} %give_back.1) | data formatting | bytes 1835008
  (3 shorter events, 0.0 us)

commit v3 on v2

v3 whole, which is shorter than its diff:
```python
import functools
import jax
import jax.numpy as jnp
from jax import lax
from jax.experimental import pallas as pl
from jax.experimental.pallas import tpu as pltpu
from jax.sharding import PartitionSpec as P

HEADS = 32
KV_HEADS = 4
D = 128
SPAN = 56
SEQ = 14336
RUNS = SEQ // SPAN
ROWS = 112
KROWS = 128
PEERS = 16
MESH = pl.DeviceIdType.MESH
LOG2E = 1.4426950408889634
SCALE = D ** -0.5 * LOG2E
HBM = pl.ANY
BLOCK = 512
TOGETHER = 16
PREP = 8
SPLIT = 4
CHUNK = 256
TILE_RUNS = 4
GROUP_RUNS = 2 * PEERS
TILES = GROUP_RUNS // TILE_RUNS
HEADS_HERE = 2
TILE_ROWS = TILE_RUNS * SPAN
M = HEADS_HERE * TILE_ROWS
SAFE = 90.0


def coords():
    outer, inner = lax.axis_index("outer"), lax.axis_index("inner")
    y, xh, core = outer // 4, (outer // 2) % 2, outer % 2
    return xh * 2 + inner % 2, y, inner // 2, core


def at(x, y, z, core):
    return ((y * 4 + (x // 2) * 2 + core), z * 2 + x % 2)


def greet(devices):
    barrier = pltpu.get_barrier_semaphore()
    for device in devices:
        pl.semaphore_signal(barrier, inc=1, device_id=device, device_id_type=MESH)
    pl.semaphore_wait(barrier, len(devices))


def group_peers(x, y, z, core):
    peers = []
    for d in range(1, PEERS):
        zz = (z + d // 4) % 4
        xx = (x // 2) * 2 + (x % 2 + (d // 2) % 2) % 2
        cc = (core + d % 2) % 2
        peers.append((xx, y, zz, cc))
    return peers


def slot_of(x, z, core):
    return z * 4 + (x % 2) * 2 + core


def gather_kernel(q_ref, k_ref, v_ref, pos_ref, qg_ref, kg_ref, vg_ref,
                  q_send, q_recv, z_send, z_recv, l_sem,
                  a_send, a_recv, b_send, b_recv, s_send, s_recv, news_ref):
    x, y, z, core = coords()
    xp, xq, xo = x + 1 - 2 * (x % 2), 3 - x, (x + 2) % 4
    yr, yl, yo = (y + 1) % 4, (y + 3) % 4, (y + 2) % 4
    peers = group_peers(x, y, z, core)
    arrays = ((k_ref, kg_ref), (v_ref, vg_ref))
    deep = (KROWS, ROWS)
    def slot(i, rows, start=0):
        return arrays[i][1].at[core, y, x, pl.ds(pl.multiple_of(z * deep[i] + start, 16), rows), :]

    def columns(i, head):
        return arrays[i][0].at[:, pl.ds(pl.multiple_of(head * D, D), D)]

    runs = pos_ref[...].astype(jnp.float32) * (1.0 / SPAN)
    lane = lax.broadcasted_iota(jnp.int32, (1, ROWS), 1)
    later = jnp.sum(jnp.where(lane == SPAN, runs, 0.0), axis=1, keepdims=True)
    news_ref[...] = jnp.zeros_like(news_ref)
    news_ref[:, :ROWS] = jnp.broadcast_to(jnp.where(lane == 1, later, runs), (KROWS - ROWS, ROWS)).astype(jnp.bfloat16)
    me = slot_of(x, z, core)
    lc = []
    for i, (src, dst) in enumerate(((columns(0, z), slot(0, ROWS)), (columns(1, z), slot(1, ROWS)),
                                    (news_ref, slot(0, KROWS - ROWS, ROWS)),
                                    (q_ref.at[:, pl.ds(pl.multiple_of(me * 256, 256), 256)], qg_ref.at[me]))):
        c = pltpu.make_async_copy(src, dst, l_sem.at[i])
        c.start()
        lc.append(c)
    greet([at(*p) for p in peers]
          + [at(xq, y, z, core), at(x, yr, z, core), at(x, yl, z, core)])

    sent = []

    def send(src, dst, ssem, rsem, to):
        c = pltpu.make_async_remote_copy(
            src_ref=src, dst_ref=dst, send_sem=ssem, recv_sem=rsem,
            device_id=at(*to), device_id_type=MESH)
        c.start()
        sent.append(c)
        return c

    def drain(keep):
        while len(sent) > keep:
            sent.pop(0).wait_send()

    zc = []
    for d in range(1, 4):
        zz = (z + d) % 4
        for i in range(2):
            zc.append(send(columns(i, zz), slot(i, ROWS), z_send.at[i, d], z_recv.at[i, d], (x, y, zz, core)))
        zc.append(send(news_ref, slot(0, KROWS - ROWS, ROWS), z_send.at[2, d], z_recv.at[2, d], (x, y, zz, core)))
    qc = []

    def ask(flip):
        for d, p in zip(range(1, PEERS), peers):
            if (d // 2) % 2 == flip:
                t = slot_of(p[0], p[2], p[3])
                qc.append(send(q_ref.at[:, pl.ds(pl.multiple_of(t * 256, 256), 256)],
                               qg_ref.at[me], q_send.at[d], q_recv.at[d], p))

    for c in lc:
        c.wait()
    for c in zc:
        c.wait_recv()
    ask(0)

    def block(i, bx, by, h=None):
        ref, half = arrays[i][1], 2 * deep[i]
        if h is None:
            return ref.at[core, by, bx]
        return ref.at[core, by, bx, pl.ds(h * half, half), :]

    sibling = (x, y, z, 1 - core)
    along_x = ("x", (xp, xq, xo))
    along_y = ("y", (yl, yr, yo))
    axes = ((along_x, along_y), (along_y, along_x))

    def move(axis, bx, by, n):
        if n == 0:
            return bx, by
        return (axis[1][n - 1], by) if axis[0] == "x" else (bx, axis[1][n - 1])

    def spread(i, axis, bx, by, ssem, rsem):
        ref = block(i, bx, by)
        if axis[0] == "x":
            targets = ((xp, y), (xq, y))
        else:
            targets = ((x, yr), (x, yl))
        return [send(ref, ref, ssem.at[k], rsem.at[k], (t[0], t[1], z, core)) for k, t in enumerate(targets)]

    def relay(i, axis, bx, by, got, ssem, rsem, then):
        out = []
        for n in (1, 2):
            got[n - 1].wait_recv()
            ux, uy = move(axis, bx, by, n)
            if axis[0] == "y":
                ref, to = block(i, ux, uy, n - 1), (x, (yr, yl)[n - 1], z, core)
                out.append(send(ref, ref, ssem.at[n + 1], rsem.at[n + 1], to))
            elif n == 1:
                ref = block(i, ux, uy)
                out.append(send(ref, ref, ssem.at[2], rsem.at[2], (xq, y, z, core)))
            then(n, ux, uy)
        return out

    sib = []

    def hand(i, n, bx, by):
        ref = block(i, bx, by)
        sib.append(send(ref, ref, s_send.at[i, n], s_recv.at[i, n], sibling))

    second = [[None] * 4, [None] * 4]

    def start_second(i, n):
        bx, by = move(axes[i][0], x, y, n)
        second[i][n] = spread(i, axes[i][1], bx, by, b_send.at[i, n], b_recv.at[i, n])
        hand(i, 4 * n, bx, by)

    first = [spread(i, axes[i][0], x, y, a_send.at[i], a_recv.at[i]) for i in range(2)]
    for i in range(2):
        start_second(i, 0)
    far = [relay(i, axes[i][0], x, y, first[i], a_send.at[i], a_recv.at[i],
                 lambda n, ux, uy, i=i: start_second(i, n)) for i in range(2)]
    ask(1)
    last = [[None] * 4, [None] * 4]

    def relay_second(i, n):
        bx, by = move(axes[i][0], x, y, n)
        last[i][n] = relay(i, axes[i][1], bx, by, second[i][n], b_send.at[i, n], b_recv.at[i, n],
                           lambda m, ux, uy: hand(i, 4 * n + m, ux, uy))

    drain(24)
    for i in range(2):
        relay_second(i, 0)
    for i in range(2):
        for c in far[i]:
            c.wait_recv()
        start_second(i, 3)
    for n in range(1, 4):
        drain(24)
        for i in range(2):
            relay_second(i, n)
    for n in range(4):
        for i in range(2):
            drain(16)
            for c in last[i][n]:
                c.wait_recv()
            hand(i, 4 * n + 3, *move(axes[i][1], *move(axes[i][0], x, y, n), 3))
    for c in qc:
        c.wait_recv()
    for c in sib:
        c.wait_recv()
    drain(0)


def gather(q, k, v, positions):
    dma = pltpu.SemaphoreType.DMA
    return pl.pallas_call(
        gather_kernel,
        out_shape=(
            jax.ShapeDtypeStruct((PEERS, ROWS, 256), jnp.bfloat16),
            jax.ShapeDtypeStruct((2, 4, 4, 4 * KROWS, D), jnp.bfloat16),
            jax.ShapeDtypeStruct((2, 4, 4, 4 * ROWS, D), jnp.bfloat16),
        ),
        in_specs=[pl.BlockSpec(memory_space=HBM)] * 3 + [pl.BlockSpec(memory_space=pltpu.VMEM)],
        out_specs=[pl.BlockSpec(memory_space=HBM)] * 3,
        scratch_shapes=[
            dma((PEERS,)), dma((PEERS,)), dma((3, 4)), dma((3, 4)), dma((4,)),
            dma((2, 4)), dma((2, 4)), dma((2, 4, 4)), dma((2, 4, 4)), dma((2, 16)), dma((2, 16)),
            pltpu.VMEM((KROWS - ROWS, D), jnp.bfloat16),
        ],
        compiler_params=pltpu.CompilerParams(collective_id=0, has_side_effects=True),
        name="gather",
    )(q, k, v, positions)


def return_kernel(o_ref, out_ref, send_sem, recv_sem, l_sem):
    x, y, z, core = coords()
    peers = group_peers(x, y, z, core)
    me = slot_of(x, z, core)
    there = out_ref.at[:, pl.ds(pl.multiple_of(me * 256, 256), 256)]
    own = pltpu.make_async_copy(o_ref.at[me], there, l_sem)
    own.start()
    greet([at(*p) for p in peers])
    copies = []
    for d, p in zip(range(1, PEERS), peers):
        c = pltpu.make_async_remote_copy(
            src_ref=o_ref.at[slot_of(p[0], p[2], p[3])], dst_ref=there,
            send_sem=send_sem.at[d], recv_sem=recv_sem.at[d],
            device_id=at(*p), device_id_type=MESH)
        c.start()
        copies.append(c)
    own.wait()
    for c in copies:
        c.wait_recv()
    for c in copies:
        c.wait_send()


def give_back(o):
    dma = pltpu.SemaphoreType.DMA
    return pl.pallas_call(
        return_kernel,
        out_shape=jax.ShapeDtypeStruct((ROWS, HEADS * D), jnp.bfloat16),
        in_specs=[pl.BlockSpec(memory_space=HBM)],
        out_specs=pl.BlockSpec(memory_space=HBM),
        scratch_shapes=[dma((PEERS,)), dma((PEERS,)), dma],
        compiler_params=pltpu.CompilerParams(collective_id=1, has_side_effects=True),
        name="give_back",
    )(o)


def half_of(ref, loc, stride=ROWS):
    pair = ref[pl.ds(pl.multiple_of((loc // 2) * stride, 16), ROWS), :].astype(jnp.float32)
    return jnp.where(loc % 2 == 1, pair[SPAN:], pair[:SPAN])


def attend_kernel(run_index, q_hbm, k_hbm, v_hbm, o_ref,
                  q_raw, k_raw, v_raw, k_sorted, v_sorted, q_tile, rel, acc, tot, top, weights, lately, part, part_tot, out32,
                  key_at, own, run_at, run_pos, blocks, sem):
    copies = []
    for src, dst in ((q_hbm, q_raw), (k_hbm, k_raw), (v_hbm, v_raw)):
        size = src.shape[0] // SPLIT
        for i in range(SPLIT):
            rows = pl.ds(i * size, size)
            copies.append(pltpu.make_async_copy(src.at[rows, :], dst.at[rows, :], sem.at[len(copies)]))
            copies[-1].start()

    my_x, my_y, _, _ = coords()
    for p in range(RUNS):
        own[p] = -1
    for loc in range(RUNS):
        key_at[run_index[loc]] = loc
    for i in range(GROUP_RUNS):
        z, x_lo, core, half = i // 8, (i // 4) % 2, (i // 2) % 2, i % 2
        loc = (core * 4 + my_y) * 32 + (my_x // 2 * 2 + x_lo) * 8 + z * 2 + half
        own[run_index[loc]] = i
    n = jnp.int32(0)
    for p in range(RUNS):
        who = own[p]
        run_at[n] = who
        run_pos[n] = p
        n = n + jnp.where(who >= 0, 1, 0)
    for c in copies:
        c.wait()

    @pl.loop(0, RUNS // 2 // PREP)
    def _(step):
        for i in range(PREP):
            j = step * PREP + i
            rows = pl.ds(pl.multiple_of(j * ROWS, 16), ROWS)
            a, b = key_at[2 * j], key_at[2 * j + 1]
            k2 = jnp.concatenate([half_of(k_raw, a, KROWS), half_of(k_raw, b, KROWS)], axis=0).astype(jnp.bfloat16)
            k_sorted[rows, :] = k2
            v2 = jnp.concatenate([half_of(v_raw, a), half_of(v_raw, b)], axis=0).astype(jnp.bfloat16)
            v_sorted[rows, :] = v2

    ones = jnp.ones((D, D), jnp.bfloat16)
    longest = None
    for i in range(SEQ // 2048):
        keys = k_sorted[i * 2048:(i + 1) * 2048, :]
        square = jnp.dot(keys * keys, ones, preferred_element_type=jnp.float32)
        square = jnp.max(square, axis=0, keepdims=True)
        longest = square if longest is None else jnp.maximum(longest, square)
    key_norm = jnp.max(longest) * 1.01

    longest = None
    for t in range(TILES):
        scaled = [half_of(q_raw, run_at[t * TILE_RUNS + r]) for r in range(TILE_RUNS)]
        whole = jnp.concatenate(scaled, axis=0).astype(jnp.bfloat16)
        for h in range(HEADS_HERE):
            x = whole[:, h * D:(h + 1) * D]
            q_tile[t * M + h * TILE_ROWS:t * M + (h + 1) * TILE_ROWS, :] = x
            square = jnp.dot(x * x, ones, preferred_element_type=jnp.float32)
            square = jnp.max(square, axis=0, keepdims=True)
            longest = square if longest is None else jnp.maximum(longest, square)
    query_norm = jnp.max(longest) * 1.01
    safe = query_norm * key_norm * (SCALE * SCALE) < SAFE * SAFE
    acc[...] = jnp.zeros_like(acc)
    tot[...] = jnp.zeros_like(tot)

    def rows_of(t):
        return pl.ds(pl.multiple_of(t * M, M), M)

    def scores(at, off, width):
        return lax.dot_general(q_tile[at, :], k_sorted[pl.ds(pl.multiple_of(off, 128), width), :],
                               (((1,), (1,)), ((), ())), preferred_element_type=jnp.float32) * SCALE

    def product(p, off, width):
        return jnp.dot(p, v_sorted[pl.ds(pl.multiple_of(off, 128), width), :],
                       preferred_element_type=jnp.float32)

    def seen(t, off):
        see = rel[t] >= off
        return jnp.concatenate([see] * HEADS_HERE, axis=0)

    def weigh(t, off, slot):
        at, total = rows_of(t), None
        for i in range(BLOCK // CHUNK):
            s = scores(at, off + i * CHUNK, CHUNK)
            for w in range(0, CHUNK, 128):
                p = jnp.where(seen(t, off + i * CHUNK + w), jnp.exp2(s[:, w:w + 128]), 0.0)
                total = p if total is None else total + p
                weights[slot, :, i * CHUNK + w:i * CHUNK + w + 128] = p.astype(jnp.bfloat16)
        lately[slot] = total

    def guarded(t, off):
        at = rows_of(t)
        s = scores(at, off, CHUNK)
        cols, vis, best = [], [], top[...]
        for w in range(CHUNK // 128):
            see = seen(t, off + w * 128)
            col = jnp.where(see, s[:, w * 128:(w + 1) * 128], -1e30)
            cols.append(col)
            vis.append(see)
            best = jnp.maximum(best, jnp.max(col, axis=1, keepdims=True))
        fade = jnp.exp2(top[...] - best)
        top[...] = best
        total = tot[at, :] * fade
        parts = []
        for col, see in zip(cols, vis):
            p = jnp.where(see, jnp.exp2(col - best), 0.0)
            total = total + p
            parts.append(p.astype(jnp.bfloat16))
        tot[at, :] = total
        acc[at, :] = acc[at, :] * fade + product(jnp.concatenate(parts, axis=1), off, CHUNK)

    count = jnp.int32(0)
    for t in range(TILES):
        for r in range(TILE_RUNS):
            first = run_pos[t * TILE_RUNS + r] * SPAN
            rel[t, r * SPAN:(r + 1) * SPAN, :] = (lax.broadcasted_iota(jnp.int32, (SPAN, 128), 0)
                                                  - lax.broadcasted_iota(jnp.int32, (SPAN, 128), 1) + first)
        high = run_pos[t * TILE_RUNS + TILE_RUNS - 1] * SPAN + SPAN
        blocks[t] = (high + BLOCK - 1) // BLOCK
        count = count + blocks[t]
    blocks[TILES] = 1
    rel[TILES] = jnp.full_like(rel[TILES], -1)
    weights[...] = jnp.zeros_like(weights)
    lately[...] = jnp.zeros_like(lately)

    def following(t, j):
        end = j + 1 >= blocks[t]
        return jnp.minimum(t + jnp.where(end, 1, 0), TILES), jnp.where(end, 0, j + 1)

    @pl.when(safe)
    def _():
        def settle(t, u):
            acc[rows_of(t), :] += part[u]
            tot[rows_of(t), :] += part_tot[u]

        def step(_, state):
            t, j, before, at = state
            tiles = []
            for u in range(TOGETHER):
                out, out_tot = product(weights[(u + 1) % 2], at, BLOCK), lately[(u + 1) % 2]
                if u:
                    same = before == tiles[-1]
                    out = out + jnp.where(same, part[u - 1], 0.0)
                    out_tot = out_tot + jnp.where(same, part_tot[u - 1], 0.0)
                part[u] = out
                part_tot[u] = out_tot
                weigh(t, j * BLOCK, u % 2)
                tiles.append(before)
                before, at = t, j * BLOCK
                t, j = following(t, j)
            for u in range(TOGETHER - 1):
                @pl.when(tiles[u] != tiles[u + 1])
                def _():
                    settle(tiles[u], u)
            settle(tiles[-1], TOGETHER - 1)
            return t, j, before, at

        zero = jnp.int32(0)
        _, _, before, at = lax.fori_loop(0, (count + TOGETHER - 1) // TOGETHER, step,
                                         (zero, zero, zero + TILES, zero))
        part[0] = product(weights[(TOGETHER + 1) % 2], at, BLOCK)
        part_tot[0] = lately[(TOGETHER + 1) % 2]
        settle(before, 0)

    @pl.when(jnp.logical_not(safe))
    def _():
        @pl.loop(0, TILES)
        def _(t):
            top[...] = jnp.full_like(top, -1e30)

            @pl.loop(0, blocks[t] * (BLOCK // CHUNK))
            def _(j):
                guarded(t, j * CHUNK)

    for t in range(TILES):
        rows = slice(t * M, (t + 1) * M)
        done = acc[rows, :] / jnp.sum(tot[rows, :], axis=1, keepdims=True)
        for r in range(TILE_RUNS):
            rows = pl.ds(pl.multiple_of(run_at[t * TILE_RUNS + r] * SPAN, 8), SPAN)
            for h in range(HEADS_HERE):
                out32[rows, h * D:(h + 1) * D] = done[h * TILE_ROWS + r * SPAN:h * TILE_ROWS + (r + 1) * SPAN]

    o_ref[...] = out32[...].astype(jnp.bfloat16)


def attend(run_index, q, k, v):
    smem = pl.BlockSpec(memory_space=pltpu.SMEM)
    rows = PEERS * ROWS
    return pl.pallas_call(
        attend_kernel,
        out_shape=jax.ShapeDtypeStruct((rows, 256), jnp.bfloat16),
        in_specs=[smem] + [pl.BlockSpec(memory_space=HBM)] * 3,
        out_specs=pl.BlockSpec(memory_space=pltpu.VMEM),
        scratch_shapes=[
            pltpu.VMEM((rows, 256), jnp.bfloat16),
            pltpu.VMEM((RUNS // 2 * KROWS, D), jnp.bfloat16),
            pltpu.VMEM((SEQ, D), jnp.bfloat16),
            pltpu.VMEM((SEQ, D), jnp.bfloat16),
            pltpu.VMEM((SEQ, D), jnp.bfloat16),
            pltpu.VMEM((TILES * M + M, D), jnp.bfloat16),
            pltpu.VMEM((TILES + 1, TILE_ROWS, 128), jnp.int32),
            pltpu.VMEM((TILES * M + M, D), jnp.float32),
            pltpu.VMEM((TILES * M + M, 128), jnp.float32),
            pltpu.VMEM((M, 128), jnp.float32),
            pltpu.VMEM((2, M, BLOCK), jnp.bfloat16),
            pltpu.VMEM((2, M, 128), jnp.float32),
            pltpu.VMEM((TOGETHER, M, D), jnp.float32),
            pltpu.VMEM((TOGETHER, M, 128), jnp.float32),
            pltpu.VMEM((rows, 256), jnp.float32),
            pltpu.SMEM((RUNS,), jnp.int32),
            pltpu.SMEM((RUNS,), jnp.int32),
            pltpu.SMEM((GROUP_RUNS + 1,), jnp.int32),
            pltpu.SMEM((GROUP_RUNS + 1,), jnp.int32),
            pltpu.SMEM((TILES + 1,), jnp.int32),
            pltpu.SemaphoreType.DMA((3 * SPLIT,)),
        ],
        compiler_params=pltpu.CompilerParams(vmem_limit_bytes=56 << 20),
        name="attend",
    )(run_index, q, k, v)


def on_device(queries, keys, values, positions):
    qg, kg, vg = gather(queries, keys, values, positions.reshape(1, ROWS))
    run_index = kg.reshape(RUNS // 2, KROWS, D)[:, ROWS, :2].astype(jnp.int32).reshape(RUNS)
    o = attend(run_index, qg.reshape(PEERS * ROWS, 256),
               kg.reshape(RUNS // 2 * KROWS, D), vg.reshape(SEQ, D))
    return give_back(o.reshape(PEERS, ROWS, 256))


def solution(mesh):
    return jax.shard_map(
        on_device,
        mesh=mesh,
        in_specs=(
            P(("outer", "inner"), None),
            P(("outer", "inner"), None),
            P(("outer", "inner"), None),
            P(("outer", "inner")),
        ),
        out_specs=P(("outer", "inner"), None),
        check_vma=False,
    )
```

time: 214 us -> 210 us (0.981)
  no operation moved by 1% of the time
where the time goes in v3:
time: 210 us
  Pallas kernels  206 us (98%)
  local copies, waits for them, and re-layouts  3.82 us (2%)
    pallas_call x1, Pallas kernels, attend(): pl.pallas_call(attend_kernel, out_shape=jax.ShapeDtypeStruct((rows, 256),...  146 us
    pallas_call x1, Pallas kernels, gather(): pl.pallas_call(gather_kernel, out_shape=(jax.ShapeDtypeStruct((PEERS, ROW...  44.5 us
    pallas_call x1, Pallas kernels, give_back(): pl.pallas_call(return_kernel, out_shape=jax.ShapeDtypeStruct((ROWS, HEADS...  15 us

profile of v3, /device:TPU:9, one launch (start us, length us, event | category | flops | bytes accessed | tf_op | source)
XLA Modules:
  0.0 209.7 jit_solution(11243502272578076212)
XLA Ops:
  0.0 44.5 %gather.1 = (bf16[16,112,256]{2,1,0:T(8,128)(2,1)}, bf16[2,4,4,512,128]{4,3,2,1,0:T(8,128)(2,1)}, bf16[2,4,4,448,128]{4,3,2,1,0:T(8,128)(2,1)}) custom-call(bf16[112,4096]{1,0:T(8,128)(2,1)} %q_ref.1, bf16[112,512]{1,0:T(8,128)(2,1)} %k_ref.1, bf16[112,512]{1,0:T(8,128)(2,1)} %v_ref.1, s32[1,112]{1,0:T(1,128)} %bitcast.13), custom_call_target="tpu_custom_call" | custom-call | tf_op jit(solution)/shard_map/gather/pallas_call | solution.py:223
  44.5 1.0 slice.4
  45.5 0.7 reshape.28.run_index
  46.2 146.4 %attend.1 = bf16[1792,256]{1,0:T(8,128)(2,1)} custom-call(s32[256]{0:T(256)} %reshape.28.run_index, bf16[1792,256]{1,0:T(8,128)(2,1)} %bitcast.12, bf16[16384,128]{1,0:T(8,128)(2,1)} %bitcast.9, bf16[14336,128]{1,0:T(8,128)(2,1)} %bitcast.11), custom_call_target="tpu_custom_call" | custom-call | tf_op jit(solution)/shard_map/attend/pallas_call | solution.py:470
  192.6 15.0 %give_back.1 = bf16[112,4096]{1,0:T(8,128)(2,1)} custom-call(bf16[16,112,256]{2,1,0:T(8,128)(2,1)} %bitcast.10), custom_call_target="tpu_custom_call" | custom-call | tf_op jit(solution)/shard_map/give_back/pallas_call | solution.py:267
  207.6 2.2 %copy.9 = bf16[112,4096]{1,0:T(8,128)(2,1)} copy(bf16[112,4096]{1,0:T(8,128)(2,1)} %give_back.1) | data formatting | bytes 1835008
  (1 shorter events, 0.0 us)

commit v4 on v3

--- a/solution.py
+++ b/solution.py
@@ -21,6 +21,7 @@
 HBM = pl.ANY
 BLOCK = 512
 TOGETHER = 16
+FEW = 4
 PREP = 8
 SPLIT = 4
 CHUNK = 256
@@ -93,7 +94,7 @@
         c.start()
         lc.append(c)
     greet([at(*p) for p in peers]
-          + [at(xq, y, z, core), at(x, yr, z, core), at(x, yl, z, core)])
+          + [at(xq, y, z, core), at(xo, y, z, core), at(x, yr, z, core), at(x, yl, z, core), at(x, yo, z, core)])
 
     sent = []
 
@@ -146,23 +147,21 @@
             return bx, by
         return (axis[1][n - 1], by) if axis[0] == "x" else (bx, axis[1][n - 1])
 
-    def spread(i, axis, bx, by, ssem, rsem):
+    def spread(i, axis, bx, by, ssem, rsem, direct):
         ref = block(i, bx, by)
-        if axis[0] == "x":
-            targets = ((xp, y), (xq, y))
-        else:
-            targets = ((x, yr), (x, yl))
-        return [send(ref, ref, ssem.at[k], rsem.at[k], (t[0], t[1], z, core)) for k, t in enumerate(targets)]
+        targets = ((xp, y), (xq, y), (xo, y)) if axis[0] == "x" else ((x, yr), (x, yl), (x, yo))
+        return [send(ref, ref, ssem.at[k], rsem.at[k], (t[0], t[1], z, core))
+                for k, t in enumerate(targets[:3 if direct else 2])]
 
     def relay(i, axis, bx, by, got, ssem, rsem, then):
-        out = []
+        out = got[2:]
         for n in (1, 2):
             got[n - 1].wait_recv()
             ux, uy = move(axis, bx, by, n)
-            if axis[0] == "y":
+            if len(got) == 2 and axis[0] == "y":
                 ref, to = block(i, ux, uy, n - 1), (x, (yr, yl)[n - 1], z, core)
                 out.append(send(ref, ref, ssem.at[n + 1], rsem.at[n + 1], to))
-            elif n == 1:
+            elif len(got) == 2 and n == 1:
                 ref = block(i, ux, uy)
                 out.append(send(ref, ref, ssem.at[2], rsem.at[2], (xq, y, z, core)))
             then(n, ux, uy)
@@ -178,10 +177,10 @@
 
     def start_second(i, n):
         bx, by = move(axes[i][0], x, y, n)
-        second[i][n] = spread(i, axes[i][1], bx, by, b_send.at[i, n], b_recv.at[i, n])
+        second[i][n] = spread(i, axes[i][1], bx, by, b_send.at[i, n], b_recv.at[i, n], n == 3)
         hand(i, 4 * n, bx, by)
 
-    first = [spread(i, axes[i][0], x, y, a_send.at[i], a_recv.at[i]) for i in range(2)]
+    first = [spread(i, axes[i][0], x, y, a_send.at[i], a_recv.at[i], False) for i in range(2)]
     for i in range(2):
         start_second(i, 0)
     far = [relay(i, axes[i][0], x, y, first[i], a_send.at[i], a_recv.at[i],
@@ -414,33 +413,38 @@
             acc[rows_of(t), :] += part[u]
             tot[rows_of(t), :] += part_tot[u]
 
-        def step(_, state):
-            t, j, before, at = state
-            tiles = []
-            for u in range(TOGETHER):
-                out, out_tot = product(weights[(u + 1) % 2], at, BLOCK), lately[(u + 1) % 2]
-                if u:
-                    same = before == tiles[-1]
-                    out = out + jnp.where(same, part[u - 1], 0.0)
-                    out_tot = out_tot + jnp.where(same, part_tot[u - 1], 0.0)
-                part[u] = out
-                part_tot[u] = out_tot
-                weigh(t, j * BLOCK, u % 2)
-                tiles.append(before)
-                before, at = t, j * BLOCK
-                t, j = following(t, j)
-            for u in range(TOGETHER - 1):
-                @pl.when(tiles[u] != tiles[u + 1])
-                def _():
-                    settle(tiles[u], u)
-            settle(tiles[-1], TOGETHER - 1)
-            return t, j, before, at
+        def steps(together):
+            def step(_, state):
+                t, j, before, at = state
+                tiles = []
+                for u in range(together):
+                    out, out_tot = product(weights[(u + 1) % 2], at, BLOCK), lately[(u + 1) % 2]
+                    if u:
+                        same = before == tiles[-1]
+                        out = out + jnp.where(same, part[u - 1], 0.0)
+                        out_tot = out_tot + jnp.where(same, part_tot[u - 1], 0.0)
+                    part[u] = out
+                    part_tot[u] = out_tot
+                    weigh(t, j * BLOCK, u % 2)
+                    tiles.append(before)
+                    before, at = t, j * BLOCK
+                    t, j = following(t, j)
+                for u in range(together - 1):
+                    @pl.when(tiles[u] != tiles[u + 1])
+                    def _():
+                        settle(tiles[u], u)
+                settle(tiles[-1], together - 1)
+                return t, j, before, at
+
+            return step
 
         zero = jnp.int32(0)
-        _, _, before, at = lax.fori_loop(0, (count + TOGETHER - 1) // TOGETHER, step,
-                                         (zero, zero, zero + TILES, zero))
-        part[0] = product(weights[(TOGETHER + 1) % 2], at, BLOCK)
-        part_tot[0] = lately[(TOGETHER + 1) % 2]
+        state = (zero, zero, zero + TILES, zero)
+        state = lax.fori_loop(0, count // TOGETHER, steps(TOGETHER), state)
+        state = lax.fori_loop(0, (count % TOGETHER + FEW - 1) // FEW, steps(FEW), state)
+        _, _, before, at = state
+        part[0] = product(weights[1], at, BLOCK)
+        part_tot[0] = lately[1]
         settle(before, 0)
 
     @pl.when(jnp.logical_not(safe))

time: 210 us -> 220 us (1.048)
  Pallas kernels: 206 us -> 216 us
    pallas_call x1, Pallas kernels: 146 us -> 158 us  [attend(): pl.pallas_call(attend_kernel, out_shape=jax.ShapeDtypeStruct((rows, 256),...]
where the time goes in v4:
time: 220 us
  Pallas kernels  216 us (98%)
  local copies, waits for them, and re-layouts  3.82 us (2%)
    pallas_call x1, Pallas kernels, attend(): pl.pallas_call(attend_kernel, out_shape=jax.ShapeDtypeStruct((rows, 256),...  158 us
    pallas_call x1, Pallas kernels, gather(): pl.pallas_call(gather_kernel, out_shape=(jax.ShapeDtypeStruct((PEERS, ROW...  43.2 us
    pallas_call x1, Pallas kernels, give_back(): pl.pallas_call(return_kernel, out_shape=jax.ShapeDtypeStruct((ROWS, HEADS...  15 us

profile of v4, /device:TPU:9, one launch (start us, length us, event | category | flops | bytes accessed | tf_op | source)
XLA Modules:
  0.0 220.2 jit_solution(8772237041732971250)
XLA Ops:
  0.0 43.2 %gather.1 = (bf16[16,112,256]{2,1,0:T(8,128)(2,1)}, bf16[2,4,4,512,128]{4,3,2,1,0:T(8,128)(2,1)}, bf16[2,4,4,448,128]{4,3,2,1,0:T(8,128)(2,1)}) custom-call(bf16[112,4096]{1,0:T(8,128)(2,1)} %q_ref.1, bf16[112,512]{1,0:T(8,128)(2,1)} %k_ref.1, bf16[112,512]{1,0:T(8,128)(2,1)} %v_ref.1, s32[1,112]{1,0:T(1,128)} %bitcast.13), custom_call_target="tpu_custom_call" | custom-call | tf_op jit(solution)/shard_map/gather/pallas_call | solution.py:222
  43.2 1.0 slice.4
  44.2 0.7 reshape.28.run_index
  44.9 158.1 %attend.1 = bf16[1792,256]{1,0:T(8,128)(2,1)} custom-call(s32[256]{0:T(256)} %reshape.28.run_index, bf16[1792,256]{1,0:T(8,128)(2,1)} %bitcast.12, bf16[16384,128]{1,0:T(8,128)(2,1)} %bitcast.9, bf16[14336,128]{1,0:T(8,128)(2,1)} %bitcast.11), custom_call_target="tpu_custom_call" | custom-call | tf_op jit(solution)/shard_map/attend/pallas_call | solution.py:474
  202.9 15.0 %give_back.1 = bf16[112,4096]{1,0:T(8,128)(2,1)} custom-call(bf16[16,112,256]{2,1,0:T(8,128)(2,1)} %bitcast.10), custom_call_target="tpu_custom_call" | custom-call | tf_op jit(solution)/shard_map/give_back/pallas_call | solution.py:266
  218.0 2.2 copy.9
  (1 shorter events, 0.0 us)
